TPU v7x, 32 devices: a whole 2x2x4 slice. The times are simulated.
32 devices in a mesh: mem: 8 (over y, x, core), slab: 4 (over z).
Axes of the slice: x: 2, y: 2, z: 4, core: 2. Of those that a mesh axis runs over, the one named last changes fastest.
Arguments:
- prior_sample_stack: float32 [8, 3, 16, 512], P('mem', None, None, 'slab'), may hold values from -4 to 4
- obs_cell: int32 [8, 512], P('mem', 'slab'), may hold values from 0 to 255
- obs_value: float32 [8, 512], P('mem', 'slab'), may hold values from -4 to 4
- obs_bin: int32 [8, 512], P('mem', 'slab'), may hold values from 0 to 3
Outputs:
- analysis: float32 [8, 3, 16, 512], P('mem', None, None, 'slab')
Inputs may be any that keep to these rules, and one draw needn't show every extreme that they name: obs_cell is local row times 128 plus local column within the observation's region rows and its index of slab's columns.
All inputs are finite; a program needn't handle non-finite values.
Results may differ from a plain program's by a relative error of at most 0.0003.
Values sent between devices are 32-bit elements; how exact they have to be, the bound alone decides.
No kernel may reach another device: no remote copies, remote signals or barrier semaphores. Data moves between devices by JAX's collectives and lax.ppermute only.
A program may use at most 64 MiB of HBM per device.

v0:
```python
import math

import jax
import jax.numpy as jnp
from jax import lax
from jax.sharding import PartitionSpec as P

STEPS = 12
SWEEPS = 8


time_step = 0.25
gravity = 1.0
mean_depth = 1.0
coriolis = 0.2
viscosity = 0.4
inflation = 1.1
highest = lax.Precision.HIGHEST


def padded_2(cells, sides, width):
    for axis, dim in sides:
        count = lax.axis_size(axis)
        head = lax.slice_in_dim(cells, 0, width, axis=dim)
        tail = lax.slice_in_dim(cells, cells.shape[dim] - width, cells.shape[dim], axis=dim)
        cells = jnp.concatenate(
            [
                lax.ppermute(tail, axis, [(i, (i + 1) % count) for i in range(count)]),
                cells,
                lax.ppermute(head, axis, [((i + 1) % count, i) for i in range(count)]),
            ],
            axis=dim,
        )
    return cells


def passed_along(value, axis, steps):
    count = lax.axis_size(axis)
    pairs = [(source, (source + steps) % count) for source in range(count)]
    return lax.ppermute(value, axis, pairs)


def centre(values):
    return values[:, 1:-1]


def east_of(values):
    return jnp.roll(values[:, 1:-1], -1, 0)


def west_of(values):
    return jnp.roll(values[:, 1:-1], 1, 0)


def north_of(values):
    return values[:, 2:]


def south_of(values):
    return values[:, :-2]


def spread(values):
    return (
        east_of(values)
        + west_of(values)
        + north_of(values)
        + south_of(values)
        - 4.0 * centre(values)
    )


def slope_x(values):
    return 0.5 * (east_of(values) - west_of(values))


def slope_y(values):
    return 0.5 * (north_of(values) - south_of(values))


def advance(padded):
    elevation_anomaly = padded[0]
    east_wind = padded[1]
    north_wind = padded[2]
    flux_x = (mean_depth + elevation_anomaly) * east_wind
    flux_y = (mean_depth + elevation_anomaly) * north_wind
    east_mid = centre(east_wind)
    north_mid = centre(north_wind)
    new_height = centre(elevation_anomaly) + time_step * (
        viscosity * spread(elevation_anomaly) - slope_x(flux_x) - slope_y(flux_y)
    )
    new_east = east_mid + time_step * (
        viscosity * spread(east_wind)
        - east_mid * slope_x(east_wind)
        - north_mid * slope_y(east_wind)
        - gravity * slope_x(elevation_anomaly)
        + coriolis * north_mid
    )
    new_north = north_mid + time_step * (
        viscosity * spread(north_wind)
        - east_mid * slope_x(north_wind)
        - north_mid * slope_y(north_wind)
        - gravity * slope_y(elevation_anomaly)
        - coriolis * east_mid
    )
    return jnp.stack([new_height, new_east, new_north])


def partial_sums(anomaly, distance, obs_weight, innovation, band_rows):
    target = jnp.arange(band_rows).astype(jnp.float32)
    scaled_dist = (distance[None, :] - target[:, None]) / float(band_rows)
    weight = obs_weight[None, :] * jnp.exp(-0.5 * scaled_dist * scaled_dist)
    scaled = anomaly[None, :, :] * weight[:, None, :]
    gram_matrix = jnp.einsum("tmj,kj->tmk", scaled, anomaly, precision=highest)
    pull_vector = jnp.einsum("tmj,j->tm", scaled, innovation, precision=highest)
    return (gram_matrix, pull_vector)


def batch_product(left, right):
    return jnp.einsum("tij,tjk->tik", left, right, precision=highest)


def weights_from(gram_matrix, pull_vector, members):
    identity = jnp.eye(members, dtype=jnp.float32)
    gram_matrix = gram_matrix + (members - 1) / inflation * identity[None]
    traces = jnp.trace(gram_matrix, axis1=1, axis2=2)
    iterate = gram_matrix / traces[:, None, None]
    inverse = jnp.broadcast_to(identity, gram_matrix.shape)
    for iteration in range(SWEEPS):
        correction = 1.5 * identity[None] - 0.5 * batch_product(inverse, iterate)
        iterate, inverse = (batch_product(iterate, correction), batch_product(correction, inverse))
    inv_root = inverse / jnp.sqrt(traces)[:, None, None]
    inner = jnp.einsum("tij,tj->ti", inv_root, pull_vector, precision=highest)
    mean_weights = jnp.einsum("tij,tj->ti", inv_root, inner, precision=highest)
    return math.sqrt(members - 1) * inv_root + mean_weights[:, :, None]


def apply_weights(zone_portion, mixing):
    mean_state = jnp.mean(zone_portion, axis=0)
    spread_state = zone_portion - mean_state[None]
    return mean_state[None] + jnp.einsum("mftc,tmk->kftc", spread_state, mixing, precision=highest)


def local(prior_sample_stack, obs_cell, obs_value, obs_bin):
    current_condition = prior_sample_stack[0]

    def four_steps(counter, values):
        padded = padded_2(values, (("slab", 2),), 4)
        for substep in range(4):
            padded = advance(padded)
        return padded

    current_condition = lax.fori_loop(0, STEPS // 4, four_steps, current_condition)
    predicted_grid = current_condition[None]
    zone_collection = lax.all_to_all(predicted_grid, "mem", split_axis=2, concat_axis=0, tiled=True)
    heights = zone_collection[:, 0]
    members = heights.shape[0]
    band_rows = heights.shape[1]
    columns = heights.shape[2]
    observed = jnp.take(heights.reshape(members, band_rows * columns), obs_cell[0], axis=1)
    obs_mean = jnp.mean(observed, axis=0)
    anomaly = observed - obs_mean[None]
    extras = jnp.stack(
        [
            obs_value[0] - obs_mean,
            10.0 / (1.0 + obs_bin[0].astype(jnp.float32)),
            (obs_cell[0] // columns).astype(jnp.float32),
        ]
    )
    package = (anomaly, extras)
    collected = [(0, package)]
    for stride in (1, -1, 2, -2):
        collected.append((-stride, passed_along((package[0], package[1]), "mem", stride)))
    all_anomaly = jnp.concatenate([entry[1][0] for entry in collected], axis=1)
    distance = jnp.concatenate(
        [entry[1][1][2] + float(entry[0] * band_rows) for entry in collected]
    )
    obs_weight = jnp.concatenate([entry[1][1][1] for entry in collected])
    innovation = jnp.concatenate([entry[1][1][0] for entry in collected])
    gram_matrix, pull_vector = partial_sums(
        all_anomaly, distance, obs_weight, innovation, band_rows
    )
    gram_matrix, pull_vector = lax.psum((gram_matrix, pull_vector), "slab")
    mixing = weights_from(gram_matrix, pull_vector, members)
    return lax.all_to_all(
        apply_weights(zone_collection, mixing), "mem", split_axis=0, concat_axis=2, tiled=True
    )


def solution(mesh):
    placed = (P("mem", None, None, "slab"), P("mem", "slab"), P("mem", "slab"), P("mem", "slab"))
    return jax.shard_map(
        local, mesh=mesh, in_specs=placed, out_specs=P("mem", None, None, "slab"), check_vma=False
    )
```

profile of v0, /device:TPU:0, one launch (start us, length us, event | category | flops | bytes accessed | tf_op | source)
XLA Modules:
  0.0 79.5 jit_solution(15081799389065171271)
XLA Ops:
  0.0 0.7 copy-done
  0.7 31.8 %while.10 = (s32[]{:T(128)}, f32[3,16,128]{2,1,0:T(8,128)S(1)}, s32[]{:T(128)}) while((s32[]{:T(128)}, f32[3,16,128]{2,1,0:T(8,128)S(1)}, s32[]{:T(128)}) %tuple.160), condition=%wide.region_1.2_spmd, body=%wide.region_0.1_spmd.sunk | while | flops 597890 | bytes 1707389 | solution.py:153
  0.8 5.1 %collective-permute-start = (f32[3,16,4]{2,1,0:T(8,128)S(1)}, f32[3,16,4]{2,1,0:T(8,128)S(1)}, u32[]{:S(2)}, u32[]{:S(2)}) collective-permute-start(f32[3,16,4]{2,1,0:T(8,128)S(1)} %get-tuple-element.237), channel_id=1, source_target_pairs={{1,0},{2,1},{3,2},{0,3},{5,4},{6,5},{7,6},{4,7},{9,8},{10,9},{11,1... | collective-permute-start | bytes 2312 | tf_op jit(solution)/shard_map/while/body/eval_jaxpr/ppermute | solution.py:30
  5.9 1.5 %collective-permute-done = f32[3,16,4]{2,1,0:T(8,128)S(1)} collective-permute-done((f32[3,16,4]{2,1,0:T(8,128)S(1)}, f32[3,16,4]{2,1,0:T(8,128)S(1)}, u32[]{:S(2)}, u32[]{:S(2)}) %collective-permute-start) | collective-permute-done | bytes 800 | tf_op jit(solution)/shard_map/while/body/eval_jaxpr/ppermute | solution.py:30
  7.4 4.1 %collective-permute-done.1 = f32[3,16,4]{2,1,0:T(8,128)S(1)} collective-permute-done((f32[3,16,4]{2,1,0:T(8,128)S(1)}, f32[3,16,4]{2,1,0:T(8,128)S(1)}, u32[]{:S(2)}, u32[]{:S(2)}) %collective-permute-start.1) | collective-permute-done | bytes 800 | tf_op jit(solution)/shard_map/while/body/eval_jaxpr/ppermute | solution.py:28
  14.7 2.0 %collective-permute-start.1 = (f32[3,16,4]{2,1,0:T(8,128)S(1)}, f32[3,16,4]{2,1,0:T(8,128)S(1)}, u32[]{:S(2)}, u32[]{:S(2)}) collective-permute-start(f32[3,16,4]{2,1,0:T(8,128)S(1)} %get-tuple-element.238), channel_id=1, source_target_pairs={{0,1},{1,2},{2,3},{3,0},{4,5},{5,6},{6,7},{7,4},{8,9},{9,10},{10,1... | collective-permute-start | bytes 2312 | tf_op jit(solution)/shard_map/while/body/eval_jaxpr/ppermute | solution.py:28
  16.8 1.8 %collective-permute-done = f32[3,16,4]{2,1,0:T(8,128)S(1)} collective-permute-done((f32[3,16,4]{2,1,0:T(8,128)S(1)}, f32[3,16,4]{2,1,0:T(8,128)S(1)}, u32[]{:S(2)}, u32[]{:S(2)}) %collective-permute-start) | collective-permute-done | bytes 800 | tf_op jit(solution)/shard_map/while/body/eval_jaxpr/ppermute | solution.py:30
  18.6 1.9 %collective-permute-done.1 = f32[3,16,4]{2,1,0:T(8,128)S(1)} collective-permute-done((f32[3,16,4]{2,1,0:T(8,128)S(1)}, f32[3,16,4]{2,1,0:T(8,128)S(1)}, u32[]{:S(2)}, u32[]{:S(2)}) %collective-permute-start.1) | collective-permute-done | bytes 800 | tf_op jit(solution)/shard_map/while/body/eval_jaxpr/ppermute | solution.py:28
  23.7 2.0 %collective-permute-start.1 = (f32[3,16,4]{2,1,0:T(8,128)S(1)}, f32[3,16,4]{2,1,0:T(8,128)S(1)}, u32[]{:S(2)}, u32[]{:S(2)}) collective-permute-start(f32[3,16,4]{2,1,0:T(8,128)S(1)} %get-tuple-element.238), channel_id=1, source_target_pairs={{0,1},{1,2},{2,3},{3,0},{4,5},{5,6},{6,7},{7,4},{8,9},{9,10},{10,1... | collective-permute-start | bytes 2312 | tf_op jit(solution)/shard_map/while/body/eval_jaxpr/ppermute | solution.py:28
  25.7 1.8 %collective-permute-done = f32[3,16,4]{2,1,0:T(8,128)S(1)} collective-permute-done((f32[3,16,4]{2,1,0:T(8,128)S(1)}, f32[3,16,4]{2,1,0:T(8,128)S(1)}, u32[]{:S(2)}, u32[]{:S(2)}) %collective-permute-start) | collective-permute-done | bytes 800 | tf_op jit(solution)/shard_map/while/body/eval_jaxpr/ppermute | solution.py:30
  27.5 1.9 %collective-permute-done.1 = f32[3,16,4]{2,1,0:T(8,128)S(1)} collective-permute-done((f32[3,16,4]{2,1,0:T(8,128)S(1)}, f32[3,16,4]{2,1,0:T(8,128)S(1)}, u32[]{:S(2)}, u32[]{:S(2)}) %collective-permute-start.1) | collective-permute-done | bytes 800 | tf_op jit(solution)/shard_map/while/body/eval_jaxpr/ppermute | solution.py:28
  32.5 0.6 copy.28
  33.1 3.9 %all-to-all-start = ((f32[1,3,16,128]{3,0,1,2:T(1,128)}), f32[1,3,16,128]{3,0,1,2:T(1,128)S(1)}, u32[]{:S(2)}, u32[]{:S(2)}) async-start(f32[1,3,16,128]{3,0,1,2:T(1,128)} %copy.28), calls=%async_computation | async-start | bytes 49152 | tf_op jit(solution)/shard_map/all_to_all | solution.py:155
  37.1 0.6 copy-done.3
  37.8 4.0 %all-to-all-done = f32[1,3,16,128]{3,0,1,2:T(1,128)S(1)} async-done(((f32[1,3,16,128]{3,0,1,2:T(1,128)}), f32[1,3,16,128]{3,0,1,2:T(1,128)S(1)}, u32[]{:S(2)}, u32[]{:S(2)}) %all-to-all-start) | async-done | bytes 24608 | tf_op jit(solution)/shard_map/all_to_all | solution.py:155
  41.9 0.7 gather_fusion
  42.7 0.6 copy-done.1
  43.4 2.6 %collective-permute-start.7 = (f32[3,128]{1,0:T(4,128)S(1)}, f32[3,128]{1,0:T(4,128)S(1)}, u32[]{:S(2)}, u32[]{:S(2)}) collective-permute-start(f32[3,128]{1,0:T(4,128)S(1)} %pad_maximum_fusion.26), channel_id=1, source_target_pairs={{0,28},{4,0},{8,4},{12,8},{16,12},{20,16},{24,20},{28,24},{1,29},{... | collective-permute-start | bytes 4616 | tf_op jit(solution)/shard_map/ppermute | solution.py:40
  46.0 2.9 %collective-permute-start.9 = (f32[3,128]{1,0:T(4,128)S(1)}, f32[3,128]{1,0:T(4,128)S(1)}, u32[]{:S(2)}, u32[]{:S(2)}) collective-permute-start(f32[3,128]{1,0:T(4,128)S(1)} %pad_maximum_fusion.26), channel_id=1, source_target_pairs={{0,24},{4,28},{8,0},{12,4},{16,8},{20,12},{24,16},{28,20},{1,25},{... | collective-permute-start | bytes 4616 | tf_op jit(solution)/shard_map/ppermute | solution.py:40
  49.1 2.6 %collective-permute-start.3 = (f32[8,128]{1,0:T(8,128)S(1)}, f32[8,128]{1,0:T(8,128)S(1)}, u32[]{:S(2)}, u32[]{:S(2)}) collective-permute-start(f32[8,128]{1,0:T(8,128)S(1)} %get-tuple-element.42), channel_id=1, source_target_pairs={{0,28},{4,0},{8,4},{12,8},{16,12},{20,16},{24,20},{28,24},{1,29},{... | collective-permute-start | bytes 12296 | tf_op jit(solution)/shard_map/ppermute | solution.py:40
  51.8 3.0 %collective-permute-start.5 = (f32[8,128]{1,0:T(8,128)S(1)}, f32[8,128]{1,0:T(8,128)S(1)}, u32[]{:S(2)}, u32[]{:S(2)}) collective-permute-start(f32[8,128]{1,0:T(8,128)S(1)} %get-tuple-element.42), channel_id=1, source_target_pairs={{0,24},{4,28},{8,0},{12,4},{16,8},{20,12},{24,16},{28,20},{1,25},{... | collective-permute-start | bytes 12296 | tf_op jit(solution)/shard_map/ppermute | solution.py:40
  55.0 1.3 %collective-permute-done.4 = f32[8,128]{1,0:T(8,128)S(1)} collective-permute-done((f32[8,128]{1,0:T(8,128)S(1)}, f32[8,128]{1,0:T(8,128)S(1)}, u32[]{:S(2)}, u32[]{:S(2)}) %collective-permute-start.4) | collective-permute-done | bytes 4128 | tf_op jit(solution)/shard_map/ppermute | solution.py:40
  56.3 0.2 fusion.36
  56.5 0.4 fusion.34
  56.9 8.9 %all-reduce = (f32[2,8,8]{2,1,0:T(8,128)S(1)}, f32[2,8]{1,0:T(2,128)S(1)}) all-reduce(f32[2,8,8]{2,1,0:T(8,128)S(1)} %fusion.36, f32[2,8]{1,0:T(2,128)S(1)} %bitcast.180), channel_id=1, replica_groups=mesh['mem'=8,'slab'=4] {'slab'}, use_global_device_ids=true, to_apply=%region_4.5 | all-reduce | flops 144 | bytes 1152 | tf_op jit(solution)/shard_map/psum | solution.py:183
  65.9 0.2 fusion.33
  66.1 0.2 fusion.62
  66.3 0.1 fusion.53
  66.5 0.1 fusion.32
  66.6 0.1 fusion.100
  66.9 0.1 fusion.31
  67.0 0.1 fusion.102
  67.2 0.1 fusion.101
  67.3 0.1 fusion.30
  67.5 0.1 fusion.104
  67.8 0.1 fusion.29
  67.9 0.1 fusion.106
  68.1 0.1 fusion.105
  68.2 0.1 fusion.28
  68.3 0.1 fusion.108
  68.6 0.1 fusion.27
  68.9 0.1 fusion.109
  69.1 0.1 fusion.26
  69.4 0.1 convolution_bitcast_fusion.1
  69.5 0.1 fusion.111
  69.7 0.3 fusion.25
  70.0 8.9 %all_to_all.36 = f32[8,3,2,128]{3,2,1,0:T(2,128)S(1)} all-to-all(f32[8,3,2,128]{3,2,1,0:T(2,128)S(1)} %copy.34), channel_id=1, replica_groups=mesh['mem'=8,'slab'=4] {'mem'}, dimensions={0} | all-to-all | bytes 49152 | tf_op jit(solution)/shard_map/all_to_all | solution.py:185
  78.9 0.6 copy.35
  (188 shorter events, 10.9 us)
Async XLA Ops:
  0.0 0.7 copy-start
  0.8 6.6 %collective-permute-start = (f32[3,16,4]{2,1,0:T(8,128)S(1)}, f32[3,16,4]{2,1,0:T(8,128)S(1)}, u32[]{:S(2)}, u32[]{:S(2)}) collective-permute-start(f32[3,16,4]{2,1,0:T(8,128)S(1)} %get-tuple-element.237), channel_id=1, source_target_pairs={{1,0},{2,1},{3,2},{0,3},{5,4},{6,5},{7,6},{4,7},{9,8},{10,9},{11,1... | collective-permute-start | bytes 2312 | tf_op jit(solution)/shard_map/while/body/eval_jaxpr/ppermute | solution.py:30
  5.9 5.6 %collective-permute-start.1 = (f32[3,16,4]{2,1,0:T(8,128)S(1)}, f32[3,16,4]{2,1,0:T(8,128)S(1)}, u32[]{:S(2)}, u32[]{:S(2)}) collective-permute-start(f32[3,16,4]{2,1,0:T(8,128)S(1)} %get-tuple-element.238), channel_id=1, source_target_pairs={{0,1},{1,2},{2,3},{3,0},{4,5},{5,6},{6,7},{7,4},{8,9},{9,10},{10,1... | collective-permute-start | bytes 2312 | tf_op jit(solution)/shard_map/while/body/eval_jaxpr/ppermute | solution.py:28
  14.7 3.8 %collective-permute-start = (f32[3,16,4]{2,1,0:T(8,128)S(1)}, f32[3,16,4]{2,1,0:T(8,128)S(1)}, u32[]{:S(2)}, u32[]{:S(2)}) collective-permute-start(f32[3,16,4]{2,1,0:T(8,128)S(1)} %get-tuple-element.237), channel_id=1, source_target_pairs={{1,0},{2,1},{3,2},{0,3},{5,4},{6,5},{7,6},{4,7},{9,8},{10,9},{11,1... | collective-permute-start | bytes 2312 | tf_op jit(solution)/shard_map/while/body/eval_jaxpr/ppermute | solution.py:30
  14.7 5.7 %collective-permute-start.1 = (f32[3,16,4]{2,1,0:T(8,128)S(1)}, f32[3,16,4]{2,1,0:T(8,128)S(1)}, u32[]{:S(2)}, u32[]{:S(2)}) collective-permute-start(f32[3,16,4]{2,1,0:T(8,128)S(1)} %get-tuple-element.238), channel_id=1, source_target_pairs={{0,1},{1,2},{2,3},{3,0},{4,5},{5,6},{6,7},{7,4},{8,9},{9,10},{10,1... | collective-permute-start | bytes 2312 | tf_op jit(solution)/shard_map/while/body/eval_jaxpr/ppermute | solution.py:28
  23.7 3.8 %collective-permute-start = (f32[3,16,4]{2,1,0:T(8,128)S(1)}, f32[3,16,4]{2,1,0:T(8,128)S(1)}, u32[]{:S(2)}, u32[]{:S(2)}) collective-permute-start(f32[3,16,4]{2,1,0:T(8,128)S(1)} %get-tuple-element.237), channel_id=1, source_target_pairs={{1,0},{2,1},{3,2},{0,3},{5,4},{6,5},{7,6},{4,7},{9,8},{10,9},{11,1... | collective-permute-start | bytes 2312 | tf_op jit(solution)/shard_map/while/body/eval_jaxpr/ppermute | solution.py:30
  23.7 5.7 %collective-permute-start.1 = (f32[3,16,4]{2,1,0:T(8,128)S(1)}, f32[3,16,4]{2,1,0:T(8,128)S(1)}, u32[]{:S(2)}, u32[]{:S(2)}) collective-permute-start(f32[3,16,4]{2,1,0:T(8,128)S(1)} %get-tuple-element.238), channel_id=1, source_target_pairs={{0,1},{1,2},{2,3},{3,0},{4,5},{5,6},{6,7},{7,4},{8,9},{9,10},{10,1... | collective-permute-start | bytes 2312 | tf_op jit(solution)/shard_map/while/body/eval_jaxpr/ppermute | solution.py:28
  33.1 3.9 %copy-start.2 = (s32[1,128]{1,0:T(1,128)S(1)}, s32[1,128]{1,0:T(1,128)}, u32[]{:S(2)}) copy-start(s32[1,128]{1,0:T(1,128)} %param.7) | copy-start | bytes 1540
  33.1 8.7 %all-to-all-start = ((f32[1,3,16,128]{3,0,1,2:T(1,128)}), f32[1,3,16,128]{3,0,1,2:T(1,128)S(1)}, u32[]{:S(2)}, u32[]{:S(2)}) async-start(f32[1,3,16,128]{3,0,1,2:T(1,128)} %copy.28), calls=%async_computation | async-start | bytes 49152 | tf_op jit(solution)/shard_map/all_to_all | solution.py:155
  37.1 0.7 copy-start.3
  42.6 0.7 copy-start.1
  43.3 5.7 %collective-permute-start.6 = (f32[3,128]{1,0:T(4,128)S(1)}, f32[3,128]{1,0:T(4,128)S(1)}, u32[]{:S(2)}, u32[]{:S(2)}) collective-permute-start(f32[3,128]{1,0:T(4,128)S(1)} %pad_maximum_fusion.26), channel_id=1, source_target_pairs={{0,4},{4,8},{8,12},{12,16},{16,20},{20,24},{24,28},{28,0},{1,5},{5... | collective-permute-start | bytes 4616 | tf_op jit(solution)/shard_map/ppermute | solution.py:40
  43.4 8.3 %collective-permute-start.7 = (f32[3,128]{1,0:T(4,128)S(1)}, f32[3,128]{1,0:T(4,128)S(1)}, u32[]{:S(2)}, u32[]{:S(2)}) collective-permute-start(f32[3,128]{1,0:T(4,128)S(1)} %pad_maximum_fusion.26), channel_id=1, source_target_pairs={{0,28},{4,0},{8,4},{12,8},{16,12},{20,16},{24,20},{28,24},{1,29},{... | collective-permute-start | bytes 4616 | tf_op jit(solution)/shard_map/ppermute | solution.py:40
  46.0 5.8 %collective-permute-start.8 = (f32[3,128]{1,0:T(4,128)S(1)}, f32[3,128]{1,0:T(4,128)S(1)}, u32[]{:S(2)}, u32[]{:S(2)}) collective-permute-start(f32[3,128]{1,0:T(4,128)S(1)} %pad_maximum_fusion.26), channel_id=1, source_target_pairs={{0,8},{4,12},{8,16},{12,20},{16,24},{20,28},{24,0},{28,4},{1,9},{5... | collective-permute-start | bytes 4616 | tf_op jit(solution)/shard_map/ppermute | solution.py:40
  46.0 8.8 %collective-permute-start.9 = (f32[3,128]{1,0:T(4,128)S(1)}, f32[3,128]{1,0:T(4,128)S(1)}, u32[]{:S(2)}, u32[]{:S(2)}) collective-permute-start(f32[3,128]{1,0:T(4,128)S(1)} %pad_maximum_fusion.26), channel_id=1, source_target_pairs={{0,24},{4,28},{8,0},{12,4},{16,8},{20,12},{24,16},{28,20},{1,25},{... | collective-permute-start | bytes 4616 | tf_op jit(solution)/shard_map/ppermute | solution.py:40
  49.0 5.9 %collective-permute-start.2 = (f32[8,128]{1,0:T(8,128)S(1)}, f32[8,128]{1,0:T(8,128)S(1)}, u32[]{:S(2)}, u32[]{:S(2)}) collective-permute-start(f32[8,128]{1,0:T(8,128)S(1)} %get-tuple-element.42), channel_id=1, source_target_pairs={{0,4},{4,8},{8,12},{12,16},{16,20},{20,24},{24,28},{28,0},{1,5},{5... | collective-permute-start | bytes 12296 | tf_op jit(solution)/shard_map/ppermute | solution.py:40
  49.1 5.9 %collective-permute-start.3 = (f32[8,128]{1,0:T(8,128)S(1)}, f32[8,128]{1,0:T(8,128)S(1)}, u32[]{:S(2)}, u32[]{:S(2)}) collective-permute-start(f32[8,128]{1,0:T(8,128)S(1)} %get-tuple-element.42), channel_id=1, source_target_pairs={{0,28},{4,0},{8,4},{12,8},{16,12},{20,16},{24,20},{28,24},{1,29},{... | collective-permute-start | bytes 12296 | tf_op jit(solution)/shard_map/ppermute | solution.py:40
  51.7 4.6 %collective-permute-start.4 = (f32[8,128]{1,0:T(8,128)S(1)}, f32[8,128]{1,0:T(8,128)S(1)}, u32[]{:S(2)}, u32[]{:S(2)}) collective-permute-start(f32[8,128]{1,0:T(8,128)S(1)} %get-tuple-element.42), channel_id=1, source_target_pairs={{0,8},{4,12},{8,16},{12,20},{16,24},{20,28},{24,0},{28,4},{1,9},{5... | collective-permute-start | bytes 12296 | tf_op jit(solution)/shard_map/ppermute | solution.py:40
  51.8 4.5 %collective-permute-start.5 = (f32[8,128]{1,0:T(8,128)S(1)}, f32[8,128]{1,0:T(8,128)S(1)}, u32[]{:S(2)}, u32[]{:S(2)}) collective-permute-start(f32[8,128]{1,0:T(8,128)S(1)} %get-tuple-element.42), channel_id=1, source_target_pairs={{0,24},{4,28},{8,0},{12,4},{16,8},{20,12},{24,16},{28,20},{1,25},{... | collective-permute-start | bytes 12296 | tf_op jit(solution)/shard_map/ppermute | solution.py:40
where the time goes:
time: 79.8 us; the launch traced here: 79.5 us
  starting transfers between devices  24.3 us (30%)
  waiting for transfers between devices  18.3 us (23%)
  blocking collectives  17.8 us (22%)
  local copies, waits for them, and re-layouts  10.7 us (13%)
  matrix products  4.68 us (6%)
  other arithmetic  3.26 us (4%)
    ppermute x8, starting transfers between devices, passed_along(): return lax.ppermute(value, axis, pairs)  11.3 us
    all_to_all x1, blocking collectives, local(): lax.all_to_all(apply_weights(zone_collection, mixing), 'mem', split_axis=...  8.9 us
    psum x1, blocking collectives, local(): gram_matrix, pull_vector = lax.psum((gram_matrix, pull_vector), 'slab')  8.86 us
    ppermute x3, waiting for transfers between devices, padded_2(): lax.ppermute(tail, axis, [(i, (i + 1) % count) for i in range(count)])  7.82 us
    slice x78, local copies, waits for them, and re-layouts, east_of(): return jnp.roll(values[:, 1:-1], -1, 0)  5.86 us
    ppermute x3, waiting for transfers between devices, padded_2(): lax.ppermute(head, axis, [((i + 1) % count, i) for i in range(count)])  5.12 us
    ppermute x3, starting transfers between devices, padded_2(): lax.ppermute(head, axis, [((i + 1) % count, i) for i in range(count)])  5.06 us
    ppermute x3, starting transfers between devices, padded_2(): lax.ppermute(tail, axis, [(i, (i + 1) % count) for i in range(count)])  4.04 us
  transfers between devices with their start and end apart: 15, of which 8 were waited for; matrix products, arithmetic and copies ran while one was open for 0% of the time, Pallas kernels for 0%

commit v1 on v0

--- a/solution.py
+++ b/solution.py
@@ -3,6 +3,8 @@
 import jax
 import jax.numpy as jnp
 from jax import lax
+from jax.experimental import pallas as pl
+from jax.experimental.pallas import tpu as pltpu
 from jax.sharding import PartitionSpec as P
 
 STEPS = 12
@@ -15,6 +17,7 @@
 coriolis = 0.2
 viscosity = 0.4
 inflation = 1.1
+reach = 2
 highest = lax.Precision.HIGHEST
 
 
@@ -141,7 +144,7 @@
     return mean_state[None] + jnp.einsum("mftc,tmk->kftc", spread_state, mixing, precision=highest)
 
 
-def local(prior_sample_stack, obs_cell, obs_value, obs_bin):
+def local_general(prior_sample_stack, obs_cell, obs_value, obs_bin):
     current_condition = prior_sample_stack[0]
 
     def four_steps(counter, values):
@@ -187,7 +190,325 @@
     )
 
 
+def pack_kernel(prior_ref, cell_ref, value_ref, bin_ref, pack_ref):
+    fields, rows, columns = prior_ref.shape[1:]
+    count = cell_ref.shape[1]
+    weight = 10.0 / (1.0 + bin_ref[...].astype(jnp.float32))
+    both = jnp.concatenate(
+        [weight, weight * value_ref[...], jnp.zeros((6, count), jnp.float32)], axis=0
+    )
+    total = (pack_ref.shape[0] - fields * rows) // 2 * columns
+    at_cell = (
+        lax.broadcasted_iota(jnp.int32, (total, count), 0) == cell_ref[...]
+    ).astype(jnp.float32)
+    sums = lax.dot_general(
+        both,
+        at_cell,
+        (((1,), (1,)), ((), ())),
+        precision=highest,
+        preferred_element_type=jnp.float32,
+    )
+    for field in range(fields):
+        pack_ref[field * rows : (field + 1) * rows, :] = prior_ref[0, field]
+    base = fields * rows
+    for row in range(total // columns):
+        part = slice(row * columns, (row + 1) * columns)
+        pack_ref[base + 2 * row : base + 2 * row + 2, :] = sums[0:2, part]
+
+
+def forecast_kernel(regions, band_rows, *refs):
+    pack_refs, out_ref = refs[:-1], refs[-1]
+    slabs = len(pack_refs)
+    rows = regions * band_rows
+    columns = out_ref.shape[1]
+    width = slabs * columns
+
+    def field_of(field):
+        return [
+            jnp.concatenate(
+                [ref[pl.ds(field * rows + q, regions, stride=band_rows), :] for ref in pack_refs],
+                axis=1,
+            )
+            for q in range(band_rows)
+        ]
+
+    def east(x):
+        return [
+            x[q + 1] if q + 1 < band_rows else pltpu.roll(x[0], regions - 1, 0)
+            for q in range(band_rows)
+        ]
+
+    def west(x):
+        return [x[q - 1] if q > 0 else pltpu.roll(x[-1], 1, 0) for q in range(band_rows)]
+
+    def north(x):
+        return [pltpu.roll(part, width - 1, 1) for part in x]
+
+    def south(x):
+        return [pltpu.roll(part, 1, 1) for part in x]
+
+    keep = 1.0 - 4.0 * time_step * viscosity
+    blend = time_step * viscosity
+    half = 0.5 * time_step
+    turn = time_step * coriolis
+
+    def step(counter, state):
+        h, u, v = state
+        he, hw, hn, hs = east(h), west(h), north(h), south(h)
+        ue, uw, un, us = east(u), west(u), north(u), south(u)
+        ve, vw, vn, vs = east(v), west(v), north(v), south(v)
+        fx = [(mean_depth + a) * b for a, b in zip(h, u)]
+        fy = [(mean_depth + a) * b for a, b in zip(h, v)]
+        fe, fw, fn, fs = east(fx), west(fx), north(fy), south(fy)
+        new_h, new_u, new_v = [], [], []
+        for q in range(band_rows):
+            new_h.append(
+                keep * h[q]
+                + blend * ((he[q] + hw[q]) + (hn[q] + hs[q]))
+                - half * ((fe[q] - fw[q]) + (fn[q] - fs[q]))
+            )
+            new_u.append(
+                keep * u[q]
+                + blend * ((ue[q] + uw[q]) + (un[q] + us[q]))
+                - half
+                * (
+                    u[q] * (ue[q] - uw[q])
+                    + v[q] * (un[q] - us[q])
+                    + gravity * (he[q] - hw[q])
+                )
+                + turn * v[q]
+            )
+            new_v.append(
+                keep * v[q]
+                + blend * ((ve[q] + vw[q]) + (vn[q] + vs[q]))
+                - half
+                * (
+                    u[q] * (ve[q] - vw[q])
+                    + v[q] * (vn[q] - vs[q])
+                    + gravity * (hn[q] - hs[q])
+                )
+                - turn * u[q]
+            )
+        return new_h, new_u, new_v
+
+    h, u, v = lax.fori_loop(0, STEPS, step, tuple(field_of(field) for field in range(3)))
+    at = 0
+    for q in range(band_rows):
+        for slab in range(slabs):
+            out_ref[at : at + regions, :] = h[q][:, slab * columns : (slab + 1) * columns]
+            at += regions
+    for field in (u, v):
+        for q in range(band_rows):
+            out_ref[at : at + regions, :] = field[q][:, :columns]
+            at += regions
+    for q in range(band_rows):
+        for ref in pack_refs:
+            base = 3 * rows + 2 * q
+            out_ref[at : at + 2, :] = ref[base : base + 2, :]
+            at += 2
+
+
+def analysis_kernel(regions, band_rows, slabs, me_ref, *refs):
+    members = regions
+    pack_refs, out_ref, sums_ref, scratch_ref = refs[:members], refs[-3], refs[-2], refs[-1]
+    columns = out_ref.shape[3]
+    tall = regions
+    h_rows = band_rows * slabs * tall
+    f_rows = h_rows + 2 * band_rows * tall
+    n_sums = 2 * band_rows * slabs
+
+    me = me_ref[0]
+    for b in range(members):
+        start = pl.multiple_of((me ^ b) * n_sums, n_sums)
+        sums_ref[pl.ds(start, n_sums), :] = pack_refs[b][f_rows : f_rows + n_sums, :]
+
+    lane = lax.broadcasted_iota(jnp.int32, (tall, 128), 1)
+    per_row = []
+    for q in range(band_rows):
+        gram = [[None] * members for _ in range(members)]
+        pull = [None] * members
+        for slab in range(slabs):
+            at = (q * slabs + slab) * tall
+            h = [ref[at : at + tall, :] for ref in pack_refs]
+            mean = sum(h[1:], h[0]) * (1.0 / members)
+            a = [part - mean for part in h]
+            k = (q * slabs + slab) * 2
+            weight = sums_ref[pl.ds(k, tall, stride=n_sums), :]
+            valued = sums_ref[pl.ds(k + 1, tall, stride=n_sums), :]
+            left = valued - weight * mean
+            for i in range(members):
+                wa = weight * a[i]
+                for j in range(i, members):
+                    term = wa * a[j]
+                    gram[i][j] = term if slab == 0 else gram[i][j] + term
+                term = left * a[i]
+                pull[i] = term if slab == 0 else pull[i] + term
+        packed = jnp.zeros((tall, 128), jnp.float32)
+        for i in range(members):
+            for j in range(i, members):
+                value = jnp.sum(gram[i][j], axis=1, keepdims=True)
+                here = lane == i * members + j
+                if i != j:
+                    here = here | (lane == j * members + i)
+                packed = jnp.where(here, value, packed)
+            value = jnp.sum(pull[i], axis=1, keepdims=True)
+            packed = jnp.where(lane == members * members + i, value, packed)
+        per_row.append(packed)
+
+    targets = []
+    for t in range(band_rows):
+        total = None
+        for o in range(-reach, reach + 1):
+            near = None
+            for q in range(band_rows):
+                scaled = (o * band_rows + q - t) / float(band_rows)
+                term = math.exp(-0.5 * scaled * scaled) * per_row[q]
+                near = term if near is None else near + term
+            if o % regions:
+                near = pltpu.roll(near, (-o) % regions, 0)
+            total = near if total is None else total + near
+        targets.append(total)
+    stacked = jnp.concatenate(targets, axis=0)
+    flat_lane = lax.broadcasted_iota(jnp.int32, stacked.shape, 1)
+    on_diagonal = (flat_lane < members * members) & (flat_lane % (members + 1) == 0)
+    stacked = jnp.where(on_diagonal, stacked + (members - 1) / inflation, stacked)
+
+    turned = jnp.transpose(
+        jnp.concatenate(
+            [stacked, jnp.zeros((128 - stacked.shape[0], 128), jnp.float32)], axis=0
+        )
+    )
+    gram = [turned[i * members : (i + 1) * members, :] for i in range(members)]
+    pull = turned[members * members : members * members + members, :]
+    sub = lax.broadcasted_iota(jnp.int32, (members, 128), 0)
+
+    trace = None
+    for i in range(members):
+        part = gram[i][i : i + 1, :]
+        trace = part if trace is None else trace + part
+    live = lax.broadcasted_iota(jnp.int32, (1, 128), 1) < stacked.shape[0]
+    trace = jnp.where(live, trace, 1.0)
+    eye = [jnp.where(sub == i, 1.0, 0.0) for i in range(members)]
+
+    def across(row):
+        return jnp.broadcast_to(row, (members, 128))
+
+    def product(left, right):
+        result = []
+        for i in range(members):
+            terms = [across(left[i][k : k + 1, :]) * right[k] for k in range(members)]
+            while len(terms) > 1:
+                terms = [x + y for x, y in zip(terms[::2], terms[1::2])]
+            result.append(terms[0])
+        return result
+
+    def applied(matrix, vector):
+        terms = [across(vector[k : k + 1, :]) * matrix[k] for k in range(members)]
+        while len(terms) > 1:
+            terms = [x + y for x, y in zip(terms[::2], terms[1::2])]
+        return terms[0]
+
+    scale = 1.0 / trace
+    y = [part * across(scale) for part in gram]
+    z = None
+    for sweep in range(SWEEPS):
+        zy = y if z is None else product(z, y)
+        k = [1.5 * e - 0.5 * part for e, part in zip(eye, zy)]
+        if sweep < SWEEPS - 1:
+            y = product(y, k)
+            z = k if z is None else product(k, z)
+
+    def rooted(vector):
+        return applied(k, applied(z, vector))
+
+    root_scale = lax.rsqrt(trace)
+    mean_weight = rooted(rooted(pull)) * across(scale)
+    own = rooted(eye[0]) * across(root_scale)
+    mixing = math.sqrt(members - 1) * own + mean_weight
+
+    back = jnp.transpose(
+        jnp.concatenate([mixing, jnp.zeros((128 - members, 128), jnp.float32)], axis=0)
+    )
+    for t in range(band_rows):
+        part = back[t * regions : (t + 1) * regions, :]
+        share = [
+            jnp.broadcast_to(part[:, m : m + 1], (regions, columns)) for m in range(members)
+        ]
+        for field in range(3):
+            if field == 0:
+                at = t * slabs * tall
+            else:
+                at = h_rows + ((field - 1) * band_rows + t) * tall
+            values = [ref[at : at + tall, :] for ref in pack_refs]
+            mean = sum(values[1:], values[0]) * (1.0 / members)
+            result = mean
+            for m in range(members):
+                result = result + (values[m] - mean) * share[m]
+            out_ref[0, field, pl.ds(t, regions, stride=band_rows), :] = result
+
+
+def in_vmem(count):
+    return [pl.BlockSpec(memory_space=pltpu.VMEM)] * count
+
+
+def local_direct(prior_sample_stack, obs_cell, obs_value, obs_bin):
+    members = lax.axis_size("mem")
+    slabs = lax.axis_size("slab")
+    _, fields, rows, columns = prior_sample_stack.shape
+    regions = members
+    band_rows = rows // regions
+    pack = pl.pallas_call(
+        pack_kernel,
+        out_shape=jax.ShapeDtypeStruct((fields * rows + 2 * band_rows, columns), jnp.float32),
+        in_specs=in_vmem(4),
+        out_specs=pl.BlockSpec(memory_space=pltpu.VMEM),
+    )(prior_sample_stack, obs_cell, obs_value, obs_bin)
+    packs = [pack]
+    for ahead in range(1, slabs):
+        packs.append(lax.ppermute(pack, "slab", [((i + ahead) % slabs, i) for i in range(slabs)]))
+
+    out_rows = band_rows * slabs * regions + 2 * rows + 2 * band_rows * slabs
+    block = pl.pallas_call(
+        lambda *refs: forecast_kernel(regions, band_rows, *refs),
+        out_shape=jax.ShapeDtypeStruct((out_rows, columns), jnp.float32),
+        in_specs=in_vmem(slabs),
+        out_specs=pl.BlockSpec(memory_space=pltpu.VMEM),
+    )(*packs)
+
+    def partner(value, bits):
+        return lax.ppermute(value, "mem", [(i, i ^ bits) for i in range(members)])
+
+    blocks = [None] * members
+    blocks[0] = block
+    for b in range(2, members, 2):
+        blocks[b] = partner(block, b)
+    for b in range(0, members, 2):
+        blocks[b + 1] = partner(blocks[b], 1)
+
+    me = lax.axis_index("mem").astype(jnp.int32).reshape(1)
+    return pl.pallas_call(
+        lambda *refs: analysis_kernel(regions, band_rows, slabs, *refs),
+        out_shape=jax.ShapeDtypeStruct(prior_sample_stack.shape, jnp.float32),
+        in_specs=[pl.BlockSpec(memory_space=pltpu.SMEM)] + in_vmem(members),
+        out_specs=pl.BlockSpec(memory_space=pltpu.VMEM),
+        scratch_shapes=[
+            pltpu.VMEM((regions * 2 * band_rows * slabs, columns), jnp.float32),
+            pltpu.VMEM((members * members, 128), jnp.float32),
+        ],
+    )(me, *blocks)
+
+
 def solution(mesh):
+    members, slabs = mesh.shape["mem"], mesh.shape["slab"]
+
+    def local(prior_sample_stack, obs_cell, obs_value, obs_bin):
+        _, fields, rows, columns = prior_sample_stack.shape
+        power = members & (members - 1) == 0
+        small = members * (members + 1) <= 128 and rows <= 128 and members % 8 == 0
+        if power and small and columns == 128 and rows % members == 0:
+            return local_direct(prior_sample_stack, obs_cell, obs_value, obs_bin)
+        return local_general(prior_sample_stack, obs_cell, obs_value, obs_bin)
+
     placed = (P("mem", None, None, "slab"), P("mem", "slab"), P("mem", "slab"), P("mem", "slab"))
     return jax.shard_map(
         local, mesh=mesh, in_specs=placed, out_specs=P("mem", None, None, "slab"), check_vma=False

time: 79.8 us -> 27.2 us (0.34)
  blocking collectives: 17.8 us -> 0 us
  starting transfers between devices: 24.3 us -> 10.5 us
  waiting for transfers between devices: 18.3 us -> 7.77 us
  local copies, waits for them, and re-layouts: 10.7 us -> 1.21 us
  Pallas kernels: 0 us -> 7.37 us
  matrix products: 4.68 us -> 0 us
  other arithmetic: 3.26 us -> 0 us
    ppermute x14 -> x10, starting transfers between devices: 20.4 us -> 10.5 us  [the longest x3 6.96 us: local_direct(): lax.ppermute(pack, 'slab', [((i + ahead) % slabs, i) for i in range(slabs)])]
    all_to_all x1 -> x0, blocking collectives: 8.9 us -> none  [local(): lax.all_to_all(apply_weights(zone_collection, mixing), 'mem', split_axis=...]
    psum x1 -> x0, blocking collectives: 8.86 us -> none  [local(): gram_matrix, pull_vector = lax.psum((gram_matrix, pull_vector), 'slab')]
    pallas_call x0 -> x3, Pallas kernels: none -> 7.37 us  [the longest x1 3.15 us: local_direct(): pl.pallas_call(lambda *refs: forecast_kernel(regions, band_rows, *refs),...]
    slice x87 -> x0, local copies, waits for them, and re-layouts: 6.51 us -> none  [the longest x78 5.86 us: east_of(): return jnp.roll(values[:, 1:-1], -1, 0)]
    ppermute x14 -> x10, waiting for transfers between devices: 14.3 us -> 7.77 us  [the longest x7 5.04 us: partner(): return lax.ppermute(value, 'mem', [(i, i ^ bits) for i in range(members)])]
    dot_general x28 -> x0, matrix products: 4.68 us -> none  [the longest x23 3.47 us: batch_product(): return jnp.einsum('tij,tjk->tik', left, right, precision=highest)]
    all_to_all x1 -> x0, waiting for transfers between devices: 4 us -> none  [local(): lax.all_to_all(predicted_grid, 'mem', split_axis=2, concat_axis=0, tiled=...]
  transfers between devices with their start and end apart: 15 -> 10, of which waited for: 8 -> 8; matrix products, arithmetic and copies ran while one was open for 0% -> 0% of each run, Pallas kernels for 0% -> 0%
where the time goes in v1:
time: 27.2 us; the launch traced here: 26.9 us
  starting transfers between devices  10.5 us (39%)
  waiting for transfers between devices  7.77 us (29%)
  Pallas kernels  7.37 us (27%)
  local copies, waits for them, and re-layouts  1.21 us (4%)
    ppermute x3, starting transfers between devices, local_direct(): lax.ppermute(pack, 'slab', [((i + ahead) % slabs, i) for i in range(slabs)])  6.96 us
    ppermute x7, waiting for transfers between devices, partner(): return lax.ppermute(value, 'mem', [(i, i ^ bits) for i in range(members)])  5.04 us
    ppermute x7, starting transfers between devices, partner(): return lax.ppermute(value, 'mem', [(i, i ^ bits) for i in range(members)])  3.51 us
    pallas_call x1, Pallas kernels, local_direct(): pl.pallas_call(lambda *refs: forecast_kernel(regions, band_rows, *refs),...  3.15 us
    ppermute x3, waiting for transfers between devices, local_direct(): lax.ppermute(pack, 'slab', [((i + ahead) % slabs, i) for i in range(slabs)])  2.73 us
    pallas_call x1, Pallas kernels, local_direct(): pl.pallas_call(lambda *refs: analysis_kernel(regions, band_rows, slabs, *...  2.64 us
    pallas_call x1, Pallas kernels, local_direct(): pl.pallas_call(pack_kernel, out_shape=jax.ShapeDtypeStruct((fields * rows...  1.58 us
    unnamed x20, local copies, waits for them, and re-layouts  1.21 us
  transfers between devices with their start and end apart: 10, of which 8 were waited for; matrix products, arithmetic and copies ran while one was open for 0% of the time, Pallas kernels for 0%

profile of v1, /device:TPU:0, one launch (start us, length us, event | category | flops | bytes accessed | tf_op | source)
XLA Modules:
  0.0 26.9 jit_solution(10451281477333106435)
XLA Ops:
  0.0 1.6 %shard_map.46.refs_0_ = f32[52,128]{1,0:T(8,128)} custom-call(f32[1,3,16,128]{3,2,1,0:T(8,128)} %prior_ref.1, s32[1,128]{1,0:T(1,128)} %cell_ref.1, f32[1,128]{1,0:T(1,128)} %value_ref.1, s32[1,128]{1,0:T(1,128)} %bin_ref.1), custom_call_target="tpu_custom_call" | custom-call | tf_op jit(solution)/shard_map/pallas_call | solution.py:460
  1.6 3.0 %collective-permute-start.2 = (f32[52,128]{1,0:T(8,128)}, f32[52,128]{1,0:T(8,128)S(1)}, u32[]{:S(2)}, u32[]{:S(2)}) collective-permute-start(f32[52,128]{1,0:T(8,128)} %shard_map.46.refs_0_), channel_id=1, source_target_pairs={{3,0},{0,1},{1,2},{2,3},{7,4},{4,5},{5,6},{6,7},{11,8},{8,9},{9,10... | collective-permute-start | bytes 79880 | tf_op jit(solution)/shard_map/ppermute | solution.py:468
  4.6 2.6 %collective-permute-start.1 = (f32[52,128]{1,0:T(8,128)}, f32[52,128]{1,0:T(8,128)S(1)}, u32[]{:S(2)}, u32[]{:S(2)}) collective-permute-start(f32[52,128]{1,0:T(8,128)} %shard_map.46.refs_0_), channel_id=1, source_target_pairs={{2,0},{3,1},{0,2},{1,3},{6,4},{7,5},{4,6},{5,7},{10,8},{11,9},{8,1... | collective-permute-start | bytes 79880 | tf_op jit(solution)/shard_map/ppermute | solution.py:468
  7.2 1.3 %collective-permute-start = (f32[52,128]{1,0:T(8,128)}, f32[52,128]{1,0:T(8,128)S(1)}, u32[]{:S(2)}, u32[]{:S(2)}) collective-permute-start(f32[52,128]{1,0:T(8,128)} %shard_map.46.refs_0_), channel_id=1, source_target_pairs={{1,0},{2,1},{3,2},{0,3},{5,4},{6,5},{7,6},{4,7},{9,8},{10,9},{11,1... | collective-permute-start | bytes 79880 | tf_op jit(solution)/shard_map/ppermute | solution.py:468
  8.5 0.1 collective-permute-done.2.refs_3_
  8.7 0.0 copy-start.7
  8.7 1.2 %collective-permute-done.1.refs_2_ = f32[52,128]{1,0:T(8,128)S(1)} collective-permute-done((f32[52,128]{1,0:T(8,128)}, f32[52,128]{1,0:T(8,128)S(1)}, u32[]{:S(2)}, u32[]{:S(2)}) %collective-permute-start.1) | collective-permute-done | bytes 26656 | tf_op jit(solution)/shard_map/ppermute | solution.py:468
  9.9 0.0 copy-start.8
  9.9 1.4 %collective-permute-done.refs_1_ = f32[52,128]{1,0:T(8,128)S(1)} collective-permute-done((f32[52,128]{1,0:T(8,128)}, f32[52,128]{1,0:T(8,128)S(1)}, u32[]{:S(2)}, u32[]{:S(2)}) %collective-permute-start) | collective-permute-done | bytes 26656 | tf_op jit(solution)/shard_map/ppermute | solution.py:468
  11.3 0.0 copy-done.7
  11.3 0.0 copy-done.8
  11.3 0.0 copy-start.9
  11.3 0.6 %copy-done.9 = f32[52,128]{1,0:T(8,128)} copy-done((f32[52,128]{1,0:T(8,128)}, f32[52,128]{1,0:T(8,128)S(1)}, u32[]{:S(2)}) %copy-start.9) | copy-done | bytes 26648
  11.9 3.1 %shard_map.47.refs_1_ = f32[112,128]{1,0:T(8,128)} custom-call(f32[52,128]{1,0:T(8,128)} %shard_map.46.refs_0_, f32[52,128]{1,0:T(8,128)} %copy-done.9, f32[52,128]{1,0:T(8,128)} %copy-done.8, f32[52,128]{1,0:T(8,128)} %copy-done.7), custom_call_target="tpu_custom_call" | custom-call | tf_op jit(solution)/shard_map/pallas_call | solution.py:471
  15.0 2.4 %collective-permute-start.8 = (f32[112,128]{1,0:T(8,128)}, f32[112,128]{1,0:T(8,128)S(1)}, u32[]{:S(2)}, u32[]{:S(2)}) collective-permute-start(f32[112,128]{1,0:T(8,128)} %shard_map.47.refs_1_), channel_id=1, source_target_pairs={{0,24},{4,28},{8,16},{12,20},{16,8},{20,12},{24,0},{28,4},{1,25},{... | collective-permute-start | bytes 172040 | tf_op jit(solution)/shard_map/ppermute | solution.py:479
  17.5 0.5 %collective-permute-start.6 = (f32[112,128]{1,0:T(8,128)}, f32[112,128]{1,0:T(8,128)S(1)}, u32[]{:S(2)}, u32[]{:S(2)}) collective-permute-start(f32[112,128]{1,0:T(8,128)} %shard_map.47.refs_1_), channel_id=1, source_target_pairs={{0,16},{4,20},{8,24},{12,28},{16,0},{20,4},{24,8},{28,12},{1,17},{... | collective-permute-start | bytes 172040 | tf_op jit(solution)/shard_map/ppermute | solution.py:479
  18.0 0.5 %collective-permute-start.4 = (f32[112,128]{1,0:T(8,128)}, f32[112,128]{1,0:T(8,128)S(1)}, u32[]{:S(2)}, u32[]{:S(2)}) collective-permute-start(f32[112,128]{1,0:T(8,128)} %shard_map.47.refs_1_), channel_id=1, source_target_pairs={{0,8},{4,12},{8,0},{12,4},{16,24},{20,28},{24,16},{28,20},{1,9},{5... | collective-permute-start | bytes 172040 | tf_op jit(solution)/shard_map/ppermute | solution.py:479
  18.5 0.0 collective-permute-start.3
  18.5 2.3 %collective-permute-done.8.refs_7_ = f32[112,128]{1,0:T(8,128)S(1)} collective-permute-done((f32[112,128]{1,0:T(8,128)}, f32[112,128]{1,0:T(8,128)S(1)}, u32[]{:S(2)}, u32[]{:S(2)}) %collective-permute-start.8) | collective-permute-done | bytes 57376 | tf_op jit(solution)/shard_map/ppermute | solution.py:479
  20.8 0.0 copy-start
  20.8 0.0 collective-permute-start.9
  20.8 1.1 %collective-permute-done.6.refs_5_ = f32[112,128]{1,0:T(8,128)S(1)} collective-permute-done((f32[112,128]{1,0:T(8,128)}, f32[112,128]{1,0:T(8,128)S(1)}, u32[]{:S(2)}, u32[]{:S(2)}) %collective-permute-start.6) | collective-permute-done | bytes 57376 | tf_op jit(solution)/shard_map/ppermute | solution.py:479
  21.9 0.0 copy-start.1
  21.9 0.0 collective-permute-start.7
  21.9 0.5 %collective-permute-done.4.refs_3_ = f32[112,128]{1,0:T(8,128)S(1)} collective-permute-done((f32[112,128]{1,0:T(8,128)}, f32[112,128]{1,0:T(8,128)S(1)}, u32[]{:S(2)}, u32[]{:S(2)}) %collective-permute-start.4) | collective-permute-done | bytes 57376 | tf_op jit(solution)/shard_map/ppermute | solution.py:479
  22.4 0.0 copy-start.2
  22.4 0.0 collective-permute-start.5
  22.4 0.0 collective-permute-done.3.refs_2_
  22.4 0.0 copy-start.3
  22.4 0.0 collective-permute-done.9.refs_8_
  22.4 0.0 copy-start.4
  22.4 0.7 %collective-permute-done.7.refs_6_ = f32[112,128]{1,0:T(8,128)S(1)} collective-permute-done((f32[112,128]{1,0:T(8,128)S(1)}, f32[112,128]{1,0:T(8,128)S(1)}, u32[]{:S(2)}, u32[]{:S(2)}) %collective-permute-start.7) | collective-permute-done | bytes 57376 | tf_op jit(solution)/shard_map/ppermute | solution.py:479
  23.1 0.0 copy-start.5
  23.1 0.5 %collective-permute-done.5.refs_4_ = f32[112,128]{1,0:T(8,128)S(1)} collective-permute-done((f32[112,128]{1,0:T(8,128)S(1)}, f32[112,128]{1,0:T(8,128)S(1)}, u32[]{:S(2)}, u32[]{:S(2)}) %collective-permute-start.5) | collective-permute-done | bytes 57376 | tf_op jit(solution)/shard_map/ppermute | solution.py:479
  23.6 0.0 copy-start.6
  23.6 0.0 copy-done
  23.6 0.0 copy-done.1
  23.6 0.0 copy-done.2
  23.6 0.0 copy-done.3
  23.6 0.0 copy-done.4
  23.7 0.1 copy-done.5
  23.7 0.5 %copy-done.6 = f32[112,128]{1,0:T(8,128)} copy-done((f32[112,128]{1,0:T(8,128)}, f32[112,128]{1,0:T(8,128)S(1)}, u32[]{:S(2)}) %copy-start.6) | copy-done | bytes 57368
  24.2 2.6 %shard_map.48 = f32[1,3,16,128]{3,2,1,0:T(8,128)} custom-call(s32[1]{0:T(128)} %bitcast.refs_0_, f32[112,128]{1,0:T(8,128)} %shard_map.47.refs_1_, f32[112,128]{1,0:T(8,128)} %copy-done.3, f32[112,128]{1,0:T(8,128)} %copy-done.2, f32[112,128]{1,0:T(8,128)} %copy-done.6, f32[112,128]{1,0:T(8,128)} %copy-done.1, f32[112,128]{1,0:T(8,128)} %copy-done.5, ...), custom_call_target="tpu_custom_call" | custom-call | tf_op jit(solution)/shard_map/pallas_call | solution.py:489
Async XLA Ops:
  1.6 7.1 %collective-permute-start.2 = (f32[52,128]{1,0:T(8,128)}, f32[52,128]{1,0:T(8,128)S(1)}, u32[]{:S(2)}, u32[]{:S(2)}) collective-permute-start(f32[52,128]{1,0:T(8,128)} %shard_map.46.refs_0_), channel_id=1, source_target_pairs={{3,0},{0,1},{1,2},{2,3},{7,4},{4,5},{5,6},{6,7},{11,8},{8,9},{9,10... | collective-permute-start | bytes 79880 | tf_op jit(solution)/shard_map/ppermute | solution.py:468
  4.6 5.3 %collective-permute-start.1 = (f32[52,128]{1,0:T(8,128)}, f32[52,128]{1,0:T(8,128)S(1)}, u32[]{:S(2)}, u32[]{:S(2)}) collective-permute-start(f32[52,128]{1,0:T(8,128)} %shard_map.46.refs_0_), channel_id=1, source_target_pairs={{2,0},{3,1},{0,2},{1,3},{6,4},{7,5},{4,6},{5,7},{10,8},{11,9},{8,1... | collective-permute-start | bytes 79880 | tf_op jit(solution)/shard_map/ppermute | solution.py:468
  7.2 4.1 %collective-permute-start = (f32[52,128]{1,0:T(8,128)}, f32[52,128]{1,0:T(8,128)S(1)}, u32[]{:S(2)}, u32[]{:S(2)}) collective-permute-start(f32[52,128]{1,0:T(8,128)} %shard_map.46.refs_0_), channel_id=1, source_target_pairs={{1,0},{2,1},{3,2},{0,3},{5,4},{6,5},{7,6},{4,7},{9,8},{10,9},{11,1... | collective-permute-start | bytes 79880 | tf_op jit(solution)/shard_map/ppermute | solution.py:468
  8.7 2.6 %copy-start.7 = (f32[52,128]{1,0:T(8,128)}, f32[52,128]{1,0:T(8,128)S(1)}, u32[]{:S(2)}) copy-start(f32[52,128]{1,0:T(8,128)S(1)} %collective-permute-done.2.refs_3_) | copy-start | bytes 79876
  9.9 1.4 %copy-start.8 = (f32[52,128]{1,0:T(8,128)}, f32[52,128]{1,0:T(8,128)S(1)}, u32[]{:S(2)}) copy-start(f32[52,128]{1,0:T(8,128)S(1)} %collective-permute-done.1.refs_2_) | copy-start | bytes 79876
  11.3 0.6 %copy-start.9 = (f32[52,128]{1,0:T(8,128)}, f32[52,128]{1,0:T(8,128)S(1)}, u32[]{:S(2)}) copy-start(f32[52,128]{1,0:T(8,128)S(1)} %collective-permute-done.refs_1_) | copy-start | bytes 79876
  15.0 5.7 %collective-permute-start.8 = (f32[112,128]{1,0:T(8,128)}, f32[112,128]{1,0:T(8,128)S(1)}, u32[]{:S(2)}, u32[]{:S(2)}) collective-permute-start(f32[112,128]{1,0:T(8,128)} %shard_map.47.refs_1_), channel_id=1, source_target_pairs={{0,24},{4,28},{8,16},{12,20},{16,8},{20,12},{24,0},{28,4},{1,25},{... | collective-permute-start | bytes 172040 | tf_op jit(solution)/shard_map/ppermute | solution.py:479
  17.5 4.4 %collective-permute-start.6 = (f32[112,128]{1,0:T(8,128)}, f32[112,128]{1,0:T(8,128)S(1)}, u32[]{:S(2)}, u32[]{:S(2)}) collective-permute-start(f32[112,128]{1,0:T(8,128)} %shard_map.47.refs_1_), channel_id=1, source_target_pairs={{0,16},{4,20},{8,24},{12,28},{16,0},{20,4},{24,8},{28,12},{1,17},{... | collective-permute-start | bytes 172040 | tf_op jit(solution)/shard_map/ppermute | solution.py:479
  18.0 4.4 %collective-permute-start.4 = (f32[112,128]{1,0:T(8,128)}, f32[112,128]{1,0:T(8,128)S(1)}, u32[]{:S(2)}, u32[]{:S(2)}) collective-permute-start(f32[112,128]{1,0:T(8,128)} %shard_map.47.refs_1_), channel_id=1, source_target_pairs={{0,8},{4,12},{8,0},{12,4},{16,24},{20,28},{24,16},{28,20},{1,9},{5... | collective-permute-start | bytes 172040 | tf_op jit(solution)/shard_map/ppermute | solution.py:479
  18.5 3.9 %collective-permute-start.3 = (f32[112,128]{1,0:T(8,128)}, f32[112,128]{1,0:T(8,128)S(1)}, u32[]{:S(2)}, u32[]{:S(2)}) collective-permute-start(f32[112,128]{1,0:T(8,128)} %shard_map.47.refs_1_), channel_id=1, source_target_pairs={{0,4},{4,0},{8,12},{12,8},{16,20},{20,16},{24,28},{28,24},{1,5},{5... | collective-permute-start | bytes 172040 | tf_op jit(solution)/shard_map/ppermute | solution.py:479
  20.8 2.8 %copy-start = (f32[112,128]{1,0:T(8,128)}, f32[112,128]{1,0:T(8,128)S(1)}, u32[]{:S(2)}) copy-start(f32[112,128]{1,0:T(8,128)S(1)} %collective-permute-done.8.refs_7_) | copy-start | bytes 172036
  20.8 1.6 %collective-permute-start.9 = (f32[112,128]{1,0:T(8,128)S(1)}, f32[112,128]{1,0:T(8,128)S(1)}, u32[]{:S(2)}, u32[]{:S(2)}) collective-permute-start(f32[112,128]{1,0:T(8,128)S(1)} %collective-permute-done.8.refs_7_), channel_id=1, source_target_pairs={{0,4},{4,0},{8,12},{12,8},{16,20},{20,16},{24,28},{28,24},{1,5},{5... | collective-permute-start | bytes 172040 | tf_op jit(solution)/shard_map/ppermute | solution.py:479
  21.9 1.8 %copy-start.1 = (f32[112,128]{1,0:T(8,128)}, f32[112,128]{1,0:T(8,128)S(1)}, u32[]{:S(2)}) copy-start(f32[112,128]{1,0:T(8,128)S(1)} %collective-permute-done.6.refs_5_) | copy-start | bytes 172036
  21.9 1.2 %collective-permute-start.7 = (f32[112,128]{1,0:T(8,128)S(1)}, f32[112,128]{1,0:T(8,128)S(1)}, u32[]{:S(2)}, u32[]{:S(2)}) collective-permute-start(f32[112,128]{1,0:T(8,128)S(1)} %collective-permute-done.6.refs_5_), channel_id=1, source_target_pairs={{0,4},{4,0},{8,12},{12,8},{16,20},{20,16},{24,28},{28,24},{1,5},{5... | collective-permute-start | bytes 172040 | tf_op jit(solution)/shard_map/ppermute | solution.py:479
  22.4 1.3 %copy-start.2 = (f32[112,128]{1,0:T(8,128)}, f32[112,128]{1,0:T(8,128)S(1)}, u32[]{:S(2)}) copy-start(f32[112,128]{1,0:T(8,128)S(1)} %collective-permute-done.4.refs_3_) | copy-start | bytes 172036
  22.4 1.2 %collective-permute-start.5 = (f32[112,128]{1,0:T(8,128)S(1)}, f32[112,128]{1,0:T(8,128)S(1)}, u32[]{:S(2)}, u32[]{:S(2)}) collective-permute-start(f32[112,128]{1,0:T(8,128)S(1)} %collective-permute-done.4.refs_3_), channel_id=1, source_target_pairs={{0,4},{4,0},{8,12},{12,8},{16,20},{20,16},{24,28},{28,24},{1,5},{5... | collective-permute-start | bytes 172040 | tf_op jit(solution)/shard_map/ppermute | solution.py:479
  22.4 1.2 %copy-start.3 = (f32[112,128]{1,0:T(8,128)}, f32[112,128]{1,0:T(8,128)S(1)}, u32[]{:S(2)}) copy-start(f32[112,128]{1,0:T(8,128)S(1)} %collective-permute-done.3.refs_2_) | copy-start | bytes 172036
  22.4 1.2 %copy-start.4 = (f32[112,128]{1,0:T(8,128)}, f32[112,128]{1,0:T(8,128)S(1)}, u32[]{:S(2)}) copy-start(f32[112,128]{1,0:T(8,128)S(1)} %collective-permute-done.9.refs_8_) | copy-start | bytes 172036
  23.1 0.6 %copy-start.5 = (f32[112,128]{1,0:T(8,128)}, f32[112,128]{1,0:T(8,128)S(1)}, u32[]{:S(2)}) copy-start(f32[112,128]{1,0:T(8,128)S(1)} %collective-permute-done.7.refs_6_) | copy-start | bytes 172036
  23.6 0.6 %copy-start.6 = (f32[112,128]{1,0:T(8,128)}, f32[112,128]{1,0:T(8,128)S(1)}, u32[]{:S(2)}) copy-start(f32[112,128]{1,0:T(8,128)S(1)} %collective-permute-done.5.refs_4_) | copy-start | bytes 172036

commit v2 on v1

--- a/solution.py
+++ b/solution.py
@@ -190,14 +190,26 @@
     )
 
 
-def pack_kernel(prior_ref, cell_ref, value_ref, bin_ref, pack_ref):
-    fields, rows, columns = prior_ref.shape[1:]
-    count = cell_ref.shape[1]
+def pack_kernel(prior_hbm, cell_hbm, value_hbm, bin_hbm, pack_ref, cell_ref, value_ref, bin_ref, sems):
+    taken, columns = prior_hbm.shape
+    count = cell_hbm.shape[1]
+    prior_copy = pltpu.make_async_copy(prior_hbm, pack_ref.at[pl.ds(0, taken), :], sems.at[0])
+    copies = [
+        pltpu.make_async_copy(source, target, sems.at[1 + i])
+        for i, (source, target) in enumerate(
+            ((cell_hbm, cell_ref), (value_hbm, value_ref), (bin_hbm, bin_ref))
+        )
+    ]
+    for copy in copies:
+        copy.start()
+    prior_copy.start()
+    for copy in copies:
+        copy.wait()
     weight = 10.0 / (1.0 + bin_ref[...].astype(jnp.float32))
     both = jnp.concatenate(
         [weight, weight * value_ref[...], jnp.zeros((6, count), jnp.float32)], axis=0
     )
-    total = (pack_ref.shape[0] - fields * rows) // 2 * columns
+    total = (pack_ref.shape[0] - taken) // 2 * columns
     at_cell = (
         lax.broadcasted_iota(jnp.int32, (total, count), 0) == cell_ref[...]
     ).astype(jnp.float32)
@@ -208,12 +220,10 @@
         precision=highest,
         preferred_element_type=jnp.float32,
     )
-    for field in range(fields):
-        pack_ref[field * rows : (field + 1) * rows, :] = prior_ref[0, field]
-    base = fields * rows
     for row in range(total // columns):
         part = slice(row * columns, (row + 1) * columns)
-        pack_ref[base + 2 * row : base + 2 * row + 2, :] = sums[0:2, part]
+        pack_ref[taken + 2 * row : taken + 2 * row + 2, :] = sums[0:2, part]
+    prior_copy.wait()
 
 
 def forecast_kernel(regions, band_rows, *refs):
@@ -310,7 +320,7 @@
 
 def analysis_kernel(regions, band_rows, slabs, me_ref, *refs):
     members = regions
-    pack_refs, out_ref, sums_ref, scratch_ref = refs[:members], refs[-3], refs[-2], refs[-1]
+    pack_refs, out_ref, sums_ref = refs[:members], refs[-2], refs[-1]
     columns = out_ref.shape[3]
     tall = regions
     h_rows = band_rows * slabs * tall
@@ -451,6 +461,9 @@
     return [pl.BlockSpec(memory_space=pltpu.VMEM)] * count
 
 
+small_grant = pltpu.CompilerParams(vmem_limit_bytes=4 * 1024 * 1024)
+
+
 def local_direct(prior_sample_stack, obs_cell, obs_value, obs_bin):
     members = lax.axis_size("mem")
     slabs = lax.axis_size("slab")
@@ -460,9 +473,26 @@
     pack = pl.pallas_call(
         pack_kernel,
         out_shape=jax.ShapeDtypeStruct((fields * rows + 2 * band_rows, columns), jnp.float32),
-        in_specs=in_vmem(4),
+        in_specs=[pl.BlockSpec(memory_space=pltpu.HBM)] * 4,
         out_specs=pl.BlockSpec(memory_space=pltpu.VMEM),
-    )(prior_sample_stack, obs_cell, obs_value, obs_bin)
+        scratch_shapes=[
+            pltpu.VMEM(obs_cell.shape, obs_cell.dtype),
+            pltpu.VMEM(obs_value.shape, obs_value.dtype),
+            pltpu.VMEM(obs_bin.shape, obs_bin.dtype),
+            pltpu.SemaphoreType.DMA((4,)),
+        ],
+        compiler_params=small_grant,
+    )(
+        *(
+            pltpu.with_memory_space_constraint(array, pltpu.HBM)
+            for array in (
+                prior_sample_stack.reshape(fields * rows, columns),
+                obs_cell,
+                obs_value,
+                obs_bin,
+            )
+        )
+    )
     packs = [pack]
     for ahead in range(1, slabs):
         packs.append(lax.ppermute(pack, "slab", [((i + ahead) % slabs, i) for i in range(slabs)]))
@@ -473,6 +503,7 @@
         out_shape=jax.ShapeDtypeStruct((out_rows, columns), jnp.float32),
         in_specs=in_vmem(slabs),
         out_specs=pl.BlockSpec(memory_space=pltpu.VMEM),
+        compiler_params=small_grant,
     )(*packs)
 
     def partner(value, bits):
@@ -491,9 +522,9 @@
         out_shape=jax.ShapeDtypeStruct(prior_sample_stack.shape, jnp.float32),
         in_specs=[pl.BlockSpec(memory_space=pltpu.SMEM)] + in_vmem(members),
         out_specs=pl.BlockSpec(memory_space=pltpu.VMEM),
+        compiler_params=small_grant,
         scratch_shapes=[
             pltpu.VMEM((regions * 2 * band_rows * slabs, columns), jnp.float32),
-            pltpu.VMEM((members * members, 128), jnp.float32),
         ],
     )(me, *blocks)
 

time: 27.2 us -> 22.4 us (0.82)
  Pallas kernels: 7.37 us -> 4.29 us
  local copies, waits for them, and re-layouts: 1.21 us -> 0 us
  waiting for transfers between devices: 7.77 us -> 7.39 us
    pallas_call x1, Pallas kernels: 3.15 us -> 1.72 us  [local_direct(): pl.pallas_call(lambda *refs: forecast_kernel(regions, band_rows, *refs),...]
    unnamed x20 -> x0, local copies, waits for them, and re-layouts: 1.21 us -> none
    pallas_call x1, Pallas kernels: 2.64 us -> 1.63 us  [local_direct(): pl.pallas_call(lambda *refs: analysis_kernel(regions, band_rows, slabs, *...]
    pallas_call x1, Pallas kernels: 1.58 us -> 0.94 us  [local_direct(): pl.pallas_call(pack_kernel, out_shape=jax.ShapeDtypeStruct((fields * rows...]
  transfers between devices with their start and end apart: 10 -> 10, of which waited for: 8 -> 7; matrix products, arithmetic and copies ran while one was open for 0% -> 0% of each run, Pallas kernels for 0% -> 0%
where the time goes in v2:
time: 22.4 us; the launch traced here: 22.3 us
  starting transfers between devices  10.6 us (47%)
  waiting for transfers between devices  7.39 us (33%)
  Pallas kernels  4.29 us (19%)
    ppermute x3, starting transfers between devices, local_direct(): lax.ppermute(pack, 'slab', [((i + ahead) % slabs, i) for i in range(slabs)])  7.01 us
    ppermute x7, waiting for transfers between devices, partner(): return lax.ppermute(value, 'mem', [(i, i ^ bits) for i in range(members)])  4.86 us
    ppermute x7, starting transfers between devices, partner(): return lax.ppermute(value, 'mem', [(i, i ^ bits) for i in range(members)])  3.57 us
    ppermute x3, waiting for transfers between devices, local_direct(): lax.ppermute(pack, 'slab', [((i + ahead) % slabs, i) for i in range(slabs)])  2.52 us
    pallas_call x1, Pallas kernels, local_direct(): pl.pallas_call(lambda *refs: forecast_kernel(regions, band_rows, *refs),...  1.72 us
    pallas_call x1, Pallas kernels, local_direct(): pl.pallas_call(lambda *refs: analysis_kernel(regions, band_rows, slabs, *...  1.63 us
    pallas_call x1, Pallas kernels, local_direct(): pl.pallas_call(pack_kernel, out_shape=jax.ShapeDtypeStruct((fields * rows...  0.94 us
  transfers between devices with their start and end apart: 10, of which 7 were waited for; matrix products, arithmetic and copies ran while one was open for 0% of the time, Pallas kernels for 0%

profile of v2, /device:TPU:0, one launch (start us, length us, event | category | flops | bytes accessed | tf_op | source)
XLA Modules:
  0.0 22.3 jit_solution(11567246180116593967)
XLA Ops:
  0.0 0.9 %shard_map.46.refs_0_ = f32[52,128]{1,0:T(8,128)S(1)} custom-call(f32[48,128]{1,0:T(8,128)} %bitcast.2, s32[1,128]{1,0:T(1,128)} %cell_hbm.1, f32[1,128]{1,0:T(1,128)} %value_hbm.1, s32[1,128]{1,0:T(1,128)} %bin_hbm.1), custom_call_target="tpu_custom_call" | custom-call | tf_op jit(solution)/shard_map/pallas_call | solution.py:473
  0.9 3.1 %collective-permute-start.2 = (f32[52,128]{1,0:T(8,128)S(1)}, f32[52,128]{1,0:T(8,128)S(1)}, u32[]{:S(2)}, u32[]{:S(2)}) collective-permute-start(f32[52,128]{1,0:T(8,128)S(1)} %shard_map.46.refs_0_), channel_id=1, source_target_pairs={{3,0},{0,1},{1,2},{2,3},{7,4},{4,5},{5,6},{6,7},{11,8},{8,9},{9,10... | collective-permute-start | bytes 79880 | tf_op jit(solution)/shard_map/ppermute | solution.py:498
  4.0 2.6 %collective-permute-start.1 = (f32[52,128]{1,0:T(8,128)S(1)}, f32[52,128]{1,0:T(8,128)S(1)}, u32[]{:S(2)}, u32[]{:S(2)}) collective-permute-start(f32[52,128]{1,0:T(8,128)S(1)} %shard_map.46.refs_0_), channel_id=1, source_target_pairs={{2,0},{3,1},{0,2},{1,3},{6,4},{7,5},{4,6},{5,7},{10,8},{11,9},{8,1... | collective-permute-start | bytes 79880 | tf_op jit(solution)/shard_map/ppermute | solution.py:498
  6.6 1.3 %collective-permute-start = (f32[52,128]{1,0:T(8,128)S(1)}, f32[52,128]{1,0:T(8,128)S(1)}, u32[]{:S(2)}, u32[]{:S(2)}) collective-permute-start(f32[52,128]{1,0:T(8,128)S(1)} %shard_map.46.refs_0_), channel_id=1, source_target_pairs={{1,0},{2,1},{3,2},{0,3},{5,4},{6,5},{7,6},{4,7},{9,8},{10,9},{11,1... | collective-permute-start | bytes 79880 | tf_op jit(solution)/shard_map/ppermute | solution.py:498
  8.0 0.0 collective-permute-done.2.refs_3_
  8.0 1.1 %collective-permute-done.1.refs_2_ = f32[52,128]{1,0:T(8,128)S(1)} collective-permute-done((f32[52,128]{1,0:T(8,128)S(1)}, f32[52,128]{1,0:T(8,128)S(1)}, u32[]{:S(2)}, u32[]{:S(2)}) %collective-permute-start.1) | collective-permute-done | bytes 26656 | tf_op jit(solution)/shard_map/ppermute | solution.py:498
  9.1 1.4 %collective-permute-done.refs_1_ = f32[52,128]{1,0:T(8,128)S(1)} collective-permute-done((f32[52,128]{1,0:T(8,128)S(1)}, f32[52,128]{1,0:T(8,128)S(1)}, u32[]{:S(2)}, u32[]{:S(2)}) %collective-permute-start) | collective-permute-done | bytes 26656 | tf_op jit(solution)/shard_map/ppermute | solution.py:498
  10.5 1.7 %shard_map.47.refs_1_ = f32[112,128]{1,0:T(8,128)S(1)} custom-call(f32[52,128]{1,0:T(8,128)S(1)} %shard_map.46.refs_0_, f32[52,128]{1,0:T(8,128)S(1)} %collective-permute-done.refs_1_, f32[52,128]{1,0:T(8,128)S(1)} %collective-permute-done.1.refs_2_, f32[52,128]{1,0:T(8,128)S(1)} %collective-permute-done.2.refs_3_), custom_call_target="tpu_custom_call" | custom-call | tf_op jit(solution)/shard_map/pallas_call | solution.py:501
  12.2 2.5 %collective-permute-start.8 = (f32[112,128]{1,0:T(8,128)S(1)}, f32[112,128]{1,0:T(8,128)S(1)}, u32[]{:S(2)}, u32[]{:S(2)}) collective-permute-start(f32[112,128]{1,0:T(8,128)S(1)} %shard_map.47.refs_1_), channel_id=1, source_target_pairs={{0,24},{4,28},{8,16},{12,20},{16,8},{20,12},{24,0},{28,4},{1,25},{... | collective-permute-start | bytes 172040 | tf_op jit(solution)/shard_map/ppermute | solution.py:510
  14.7 0.5 %collective-permute-start.6 = (f32[112,128]{1,0:T(8,128)S(1)}, f32[112,128]{1,0:T(8,128)S(1)}, u32[]{:S(2)}, u32[]{:S(2)}) collective-permute-start(f32[112,128]{1,0:T(8,128)S(1)} %shard_map.47.refs_1_), channel_id=1, source_target_pairs={{0,16},{4,20},{8,24},{12,28},{16,0},{20,4},{24,8},{28,12},{1,17},{... | collective-permute-start | bytes 172040 | tf_op jit(solution)/shard_map/ppermute | solution.py:510
  15.2 0.5 %collective-permute-start.4 = (f32[112,128]{1,0:T(8,128)S(1)}, f32[112,128]{1,0:T(8,128)S(1)}, u32[]{:S(2)}, u32[]{:S(2)}) collective-permute-start(f32[112,128]{1,0:T(8,128)S(1)} %shard_map.47.refs_1_), channel_id=1, source_target_pairs={{0,8},{4,12},{8,0},{12,4},{16,24},{20,28},{24,16},{28,20},{1,9},{5... | collective-permute-start | bytes 172040 | tf_op jit(solution)/shard_map/ppermute | solution.py:510
  15.8 0.0 collective-permute-start.3
  15.8 2.0 %collective-permute-done.8.refs_7_ = f32[112,128]{1,0:T(8,128)S(1)} collective-permute-done((f32[112,128]{1,0:T(8,128)S(1)}, f32[112,128]{1,0:T(8,128)S(1)}, u32[]{:S(2)}, u32[]{:S(2)}) %collective-permute-start.8) | collective-permute-done | bytes 57376 | tf_op jit(solution)/shard_map/ppermute | solution.py:510
  17.8 0.0 collective-permute-start.9
  17.8 1.1 %collective-permute-done.6.refs_5_ = f32[112,128]{1,0:T(8,128)S(1)} collective-permute-done((f32[112,128]{1,0:T(8,128)S(1)}, f32[112,128]{1,0:T(8,128)S(1)}, u32[]{:S(2)}, u32[]{:S(2)}) %collective-permute-start.6) | collective-permute-done | bytes 57376 | tf_op jit(solution)/shard_map/ppermute | solution.py:510
  18.9 0.0 collective-permute-start.7
  18.9 0.5 %collective-permute-done.4.refs_3_ = f32[112,128]{1,0:T(8,128)S(1)} collective-permute-done((f32[112,128]{1,0:T(8,128)S(1)}, f32[112,128]{1,0:T(8,128)S(1)}, u32[]{:S(2)}, u32[]{:S(2)}) %collective-permute-start.4) | collective-permute-done | bytes 57376 | tf_op jit(solution)/shard_map/ppermute | solution.py:510
  19.4 0.0 collective-permute-start.5
  19.4 0.0 collective-permute-done.3.refs_2_
  19.4 0.0 collective-permute-done.9.refs_8_
  19.4 0.7 %collective-permute-done.7.refs_6_ = f32[112,128]{1,0:T(8,128)S(1)} collective-permute-done((f32[112,128]{1,0:T(8,128)S(1)}, f32[112,128]{1,0:T(8,128)S(1)}, u32[]{:S(2)}, u32[]{:S(2)}) %collective-permute-start.7) | collective-permute-done | bytes 57376 | tf_op jit(solution)/shard_map/ppermute | solution.py:510
  20.1 0.5 %collective-permute-done.5.refs_4_ = f32[112,128]{1,0:T(8,128)S(1)} collective-permute-done((f32[112,128]{1,0:T(8,128)S(1)}, f32[112,128]{1,0:T(8,128)S(1)}, u32[]{:S(2)}, u32[]{:S(2)}) %collective-permute-start.5) | collective-permute-done | bytes 57376 | tf_op jit(solution)/shard_map/ppermute | solution.py:510
  20.7 1.6 %shard_map.48 = f32[1,3,16,128]{3,2,1,0:T(8,128)} custom-call(s32[1]{0:T(128)} %bitcast.refs_0_, f32[112,128]{1,0:T(8,128)S(1)} %shard_map.47.refs_1_, f32[112,128]{1,0:T(8,128)S(1)} %collective-permute-done.3.refs_2_, f32[112,128]{1,0:T(8,128)S(1)} %collective-permute-done.4.refs_3_, f32[112,128]{1,0:T(8,128)S(1)} %collective-permute-done.5.refs_4_, ...), custom_call_target="tpu_custom_call" | custom-call | tf_op jit(solution)/shard_map/pallas_call | solution.py:520
Async XLA Ops:
  0.9 7.0 %collective-permute-start.2 = (f32[52,128]{1,0:T(8,128)S(1)}, f32[52,128]{1,0:T(8,128)S(1)}, u32[]{:S(2)}, u32[]{:S(2)}) collective-permute-start(f32[52,128]{1,0:T(8,128)S(1)} %shard_map.46.refs_0_), channel_id=1, source_target_pairs={{3,0},{0,1},{1,2},{2,3},{7,4},{4,5},{5,6},{6,7},{11,8},{8,9},{9,10... | collective-permute-start | bytes 79880 | tf_op jit(solution)/shard_map/ppermute | solution.py:498
  4.0 5.1 %collective-permute-start.1 = (f32[52,128]{1,0:T(8,128)S(1)}, f32[52,128]{1,0:T(8,128)S(1)}, u32[]{:S(2)}, u32[]{:S(2)}) collective-permute-start(f32[52,128]{1,0:T(8,128)S(1)} %shard_map.46.refs_0_), channel_id=1, source_target_pairs={{2,0},{3,1},{0,2},{1,3},{6,4},{7,5},{4,6},{5,7},{10,8},{11,9},{8,1... | collective-permute-start | bytes 79880 | tf_op jit(solution)/shard_map/ppermute | solution.py:498
  6.6 3.9 %collective-permute-start = (f32[52,128]{1,0:T(8,128)S(1)}, f32[52,128]{1,0:T(8,128)S(1)}, u32[]{:S(2)}, u32[]{:S(2)}) collective-permute-start(f32[52,128]{1,0:T(8,128)S(1)} %shard_map.46.refs_0_), channel_id=1, source_target_pairs={{1,0},{2,1},{3,2},{0,3},{5,4},{6,5},{7,6},{4,7},{9,8},{10,9},{11,1... | collective-permute-start | bytes 79880 | tf_op jit(solution)/shard_map/ppermute | solution.py:498
  12.2 5.6 %collective-permute-start.8 = (f32[112,128]{1,0:T(8,128)S(1)}, f32[112,128]{1,0:T(8,128)S(1)}, u32[]{:S(2)}, u32[]{:S(2)}) collective-permute-start(f32[112,128]{1,0:T(8,128)S(1)} %shard_map.47.refs_1_), channel_id=1, source_target_pairs={{0,24},{4,28},{8,16},{12,20},{16,8},{20,12},{24,0},{28,4},{1,25},{... | collective-permute-start | bytes 172040 | tf_op jit(solution)/shard_map/ppermute | solution.py:510
  14.7 4.2 %collective-permute-start.6 = (f32[112,128]{1,0:T(8,128)S(1)}, f32[112,128]{1,0:T(8,128)S(1)}, u32[]{:S(2)}, u32[]{:S(2)}) collective-permute-start(f32[112,128]{1,0:T(8,128)S(1)} %shard_map.47.refs_1_), channel_id=1, source_target_pairs={{0,16},{4,20},{8,24},{12,28},{16,0},{20,4},{24,8},{28,12},{1,17},{... | collective-permute-start | bytes 172040 | tf_op jit(solution)/shard_map/ppermute | solution.py:510
  15.2 4.2 %collective-permute-start.4 = (f32[112,128]{1,0:T(8,128)S(1)}, f32[112,128]{1,0:T(8,128)S(1)}, u32[]{:S(2)}, u32[]{:S(2)}) collective-permute-start(f32[112,128]{1,0:T(8,128)S(1)} %shard_map.47.refs_1_), channel_id=1, source_target_pairs={{0,8},{4,12},{8,0},{12,4},{16,24},{20,28},{24,16},{28,20},{1,9},{5... | collective-permute-start | bytes 172040 | tf_op jit(solution)/shard_map/ppermute | solution.py:510
  15.8 3.7 %collective-permute-start.3 = (f32[112,128]{1,0:T(8,128)S(1)}, f32[112,128]{1,0:T(8,128)S(1)}, u32[]{:S(2)}, u32[]{:S(2)}) collective-permute-start(f32[112,128]{1,0:T(8,128)S(1)} %shard_map.47.refs_1_), channel_id=1, source_target_pairs={{0,4},{4,0},{8,12},{12,8},{16,20},{20,16},{24,28},{28,24},{1,5},{5... | collective-permute-start | bytes 172040 | tf_op jit(solution)/shard_map/ppermute | solution.py:510
  17.8 1.6 %collective-permute-start.9 = (f32[112,128]{1,0:T(8,128)S(1)}, f32[112,128]{1,0:T(8,128)S(1)}, u32[]{:S(2)}, u32[]{:S(2)}) collective-permute-start(f32[112,128]{1,0:T(8,128)S(1)} %collective-permute-done.8.refs_7_), channel_id=1, source_target_pairs={{0,4},{4,0},{8,12},{12,8},{16,20},{20,16},{24,28},{28,24},{1,5},{5... | collective-permute-start | bytes 172040 | tf_op jit(solution)/shard_map/ppermute | solution.py:510
  18.9 1.2 %collective-permute-start.7 = (f32[112,128]{1,0:T(8,128)S(1)}, f32[112,128]{1,0:T(8,128)S(1)}, u32[]{:S(2)}, u32[]{:S(2)}) collective-permute-start(f32[112,128]{1,0:T(8,128)S(1)} %collective-permute-done.6.refs_5_), channel_id=1, source_target_pairs={{0,4},{4,0},{8,12},{12,8},{16,20},{20,16},{24,28},{28,24},{1,5},{5... | collective-permute-start | bytes 172040 | tf_op jit(solution)/shard_map/ppermute | solution.py:510
  19.4 1.2 %collective-permute-start.5 = (f32[112,128]{1,0:T(8,128)S(1)}, f32[112,128]{1,0:T(8,128)S(1)}, u32[]{:S(2)}, u32[]{:S(2)}) collective-permute-start(f32[112,128]{1,0:T(8,128)S(1)} %collective-permute-done.4.refs_3_), channel_id=1, source_target_pairs={{0,4},{4,0},{8,12},{12,8},{16,20},{20,16},{24,28},{28,24},{1,5},{5... | collective-permute-start | bytes 172040 | tf_op jit(solution)/shard_map/ppermute | solution.py:510

commit v3 on v2

--- a/solution.py
+++ b/solution.py
@@ -18,6 +18,7 @@
 viscosity = 0.4
 inflation = 1.1
 reach = 2
+beside = 1
 highest = lax.Precision.HIGHEST
 
 
@@ -206,23 +207,24 @@
     for copy in copies:
         copy.wait()
     weight = 10.0 / (1.0 + bin_ref[...].astype(jnp.float32))
-    both = jnp.concatenate(
-        [weight, weight * value_ref[...], jnp.zeros((6, count), jnp.float32)], axis=0
-    )
+    parts, rest = [], jnp.concatenate([weight, weight * value_ref[...]], axis=0)
+    for _ in range(3):
+        part = rest.astype(jnp.bfloat16).astype(jnp.float32)
+        parts.append(part)
+        rest = rest - part
+    parts.append(jnp.zeros((2, count), jnp.float32))
     total = (pack_ref.shape[0] - taken) // 2 * columns
-    at_cell = (
-        lax.broadcasted_iota(jnp.int32, (total, count), 0) == cell_ref[...]
-    ).astype(jnp.float32)
+    at_cell = lax.broadcasted_iota(jnp.int32, (total, count), 0) == cell_ref[...]
     sums = lax.dot_general(
-        both,
-        at_cell,
+        jnp.concatenate(parts, axis=0).astype(jnp.bfloat16),
+        jnp.where(at_cell, 1.0, 0.0).astype(jnp.bfloat16),
         (((1,), (1,)), ((), ())),
-        precision=highest,
         preferred_element_type=jnp.float32,
     )
+    sums = sums[0:2] + (sums[2:4] + sums[4:6])
     for row in range(total // columns):
         part = slice(row * columns, (row + 1) * columns)
-        pack_ref[taken + 2 * row : taken + 2 * row + 2, :] = sums[0:2, part]
+        pack_ref[taken + 2 * row : taken + 2 * row + 2, :] = sums[:, part]
     prior_copy.wait()
 
 
@@ -267,41 +269,32 @@
         he, hw, hn, hs = east(h), west(h), north(h), south(h)
         ue, uw, un, us = east(u), west(u), north(u), south(u)
         ve, vw, vn, vs = east(v), west(v), north(v), south(v)
-        fx = [(mean_depth + a) * b for a, b in zip(h, u)]
-        fy = [(mean_depth + a) * b for a, b in zip(h, v)]
-        fe, fw, fn, fs = east(fx), west(fx), north(fy), south(fy)
         new_h, new_u, new_v = [], [], []
         for q in range(band_rows):
+            ux, uy = ue[q] - uw[q], un[q] - us[q]
+            vx, vy = ve[q] - vw[q], vn[q] - vs[q]
+            flux_x = mean_depth * ux + (he[q] * ue[q] - hw[q] * uw[q])
+            flux_y = mean_depth * vy + (hn[q] * vn[q] - hs[q] * vs[q])
             new_h.append(
                 keep * h[q]
                 + blend * ((he[q] + hw[q]) + (hn[q] + hs[q]))
-                - half * ((fe[q] - fw[q]) + (fn[q] - fs[q]))
+                - half * (flux_x + flux_y)
             )
             new_u.append(
-                keep * u[q]
+                (keep * u[q] + turn * v[q])
                 + blend * ((ue[q] + uw[q]) + (un[q] + us[q]))
-                - half
-                * (
-                    u[q] * (ue[q] - uw[q])
-                    + v[q] * (un[q] - us[q])
-                    + gravity * (he[q] - hw[q])
-                )
-                + turn * v[q]
+                - half * ((u[q] * ux + v[q] * uy) + gravity * (he[q] - hw[q]))
             )
             new_v.append(
-                keep * v[q]
+                (keep * v[q] - turn * u[q])
                 + blend * ((ve[q] + vw[q]) + (vn[q] + vs[q]))
-                - half
-                * (
-                    u[q] * (ve[q] - vw[q])
-                    + v[q] * (vn[q] - vs[q])
-                    + gravity * (hn[q] - hs[q])
-                )
-                - turn * u[q]
+                - half * ((u[q] * vx + v[q] * vy) + gravity * (hn[q] - hs[q]))
             )
         return new_h, new_u, new_v
 
-    h, u, v = lax.fori_loop(0, STEPS, step, tuple(field_of(field) for field in range(3)))
+    h, u, v = lax.fori_loop(
+        0, STEPS, step, tuple(field_of(field) for field in range(3)), unroll=STEPS
+    )
     at = 0
     for q in range(band_rows):
         for slab in range(slabs):
@@ -318,9 +311,9 @@
             at += 2
 
 
-def analysis_kernel(regions, band_rows, slabs, me_ref, *refs):
-    members = regions
-    pack_refs, out_ref, sums_ref = refs[:members], refs[-2], refs[-1]
+def analysis_kernel(order, band_rows, slabs, me_ref, *refs):
+    members = regions = len(order)
+    pack_refs, out_ref, sums_ref = [refs[order.index(b)] for b in range(members)], refs[-2], refs[-1]
     columns = out_ref.shape[3]
     tall = regions
     h_rows = band_rows * slabs * tall
@@ -329,7 +322,7 @@
 
     me = me_ref[0]
     for b in range(members):
-        start = pl.multiple_of((me ^ b) * n_sums, n_sums)
+        start = pl.multiple_of((me ^ b ^ beside) * n_sums, n_sums)
         sums_ref[pl.ds(start, n_sums), :] = pack_refs[b][f_rows : f_rows + n_sums, :]
 
     lane = lax.broadcasted_iota(jnp.int32, (tall, 128), 1)
@@ -433,7 +426,7 @@
 
     root_scale = lax.rsqrt(trace)
     mean_weight = rooted(rooted(pull)) * across(scale)
-    own = rooted(eye[0]) * across(root_scale)
+    own = rooted(eye[beside]) * across(root_scale)
     mixing = math.sqrt(members - 1) * own + mean_weight
 
     back = jnp.transpose(
@@ -493,9 +486,18 @@
             )
         )
     )
-    packs = [pack]
-    for ahead in range(1, slabs):
-        packs.append(lax.ppermute(pack, "slab", [((i + ahead) % slabs, i) for i in range(slabs)]))
+    packs = [
+        lax.ppermute(
+            pack,
+            ("mem", "slab"),
+            [
+                ((m ^ beside) * slabs + (s + ahead) % slabs, m * slabs + s)
+                for m in range(members)
+                for s in range(slabs)
+            ],
+        )
+        for ahead in range(slabs)
+    ]
 
     out_rows = band_rows * slabs * regions + 2 * rows + 2 * band_rows * slabs
     block = pl.pallas_call(
@@ -509,16 +511,16 @@
     def partner(value, bits):
         return lax.ppermute(value, "mem", [(i, i ^ bits) for i in range(members)])
 
-    blocks = [None] * members
-    blocks[0] = block
+    blocks = {0: block, 1: partner(block, 1)}
+    order = [0, 1]
     for b in range(2, members, 2):
-        blocks[b] = partner(block, b)
-    for b in range(0, members, 2):
-        blocks[b + 1] = partner(blocks[b], 1)
+        blocks[b + 1] = partner(block, b + 1)
+        blocks[b] = partner(block, b) if b == 2 else partner(blocks[b + 1], 1)
+        order += [b + 1, b]
 
     me = lax.axis_index("mem").astype(jnp.int32).reshape(1)
     return pl.pallas_call(
-        lambda *refs: analysis_kernel(regions, band_rows, slabs, *refs),
+        lambda *refs: analysis_kernel(order, band_rows, slabs, *refs),
         out_shape=jax.ShapeDtypeStruct(prior_sample_stack.shape, jnp.float32),
         in_specs=[pl.BlockSpec(memory_space=pltpu.SMEM)] + in_vmem(members),
         out_specs=pl.BlockSpec(memory_space=pltpu.VMEM),
@@ -526,7 +528,7 @@
         scratch_shapes=[
             pltpu.VMEM((regions * 2 * band_rows * slabs, columns), jnp.float32),
         ],
-    )(me, *blocks)
+    )(me, *[blocks[b] for b in order])
 
 
 def solution(mesh):

time: 22.4 us -> 20.7 us (0.924)
  waiting for transfers between devices: 7.39 us -> 3.99 us
  starting transfers between devices: 10.6 us -> 12.5 us
  Pallas kernels: 4.29 us -> 4.02 us
    ppermute x7, waiting for transfers between devices: 4.86 us -> 1.87 us  [partner(): return lax.ppermute(value, 'mem', [(i, i ^ bits) for i in range(members)])]
    ppermute x7, starting transfers between devices: 3.57 us -> 5.67 us  [partner(): return lax.ppermute(value, 'mem', [(i, i ^ bits) for i in range(members)])]
    ppermute x3 -> x4, waiting for transfers between devices: 2.52 us -> 2.12 us  [local_direct(): lax.ppermute(pack, ('mem', 'slab'), [((m ^ beside) * slabs + (s + ahead)...]
    ppermute x3 -> x4, starting transfers between devices: 7.01 us -> 6.85 us  [local_direct(): lax.ppermute(pack, ('mem', 'slab'), [((m ^ beside) * slabs + (s + ahead)...]
  transfers between devices with their start and end apart: 10 -> 11, of which waited for: 7 -> 4; matrix products, arithmetic and copies ran while one was open for 0% -> 0% of each run, Pallas kernels for 0% -> 0%
where the time goes in v3:
time: 20.7 us; the launch traced here: 20.6 us
  starting transfers between devices  12.5 us (60%)
  Pallas kernels  4.02 us (19%)
  waiting for transfers between devices  3.99 us (19%)
    ppermute x4, starting transfers between devices, local_direct(): lax.ppermute(pack, ('mem', 'slab'), [((m ^ beside) * slabs + (s + ahead)...  6.85 us
    ppermute x7, starting transfers between devices, partner(): return lax.ppermute(value, 'mem', [(i, i ^ bits) for i in range(members)])  5.67 us
    ppermute x4, waiting for transfers between devices, local_direct(): lax.ppermute(pack, ('mem', 'slab'), [((m ^ beside) * slabs + (s + ahead)...  2.12 us
    ppermute x7, waiting for transfers between devices, partner(): return lax.ppermute(value, 'mem', [(i, i ^ bits) for i in range(members)])  1.87 us
    pallas_call x1, Pallas kernels, local_direct(): pl.pallas_call(lambda *refs: analysis_kernel(order, band_rows, slabs, *re...  1.64 us
    pallas_call x1, Pallas kernels, local_direct(): pl.pallas_call(lambda *refs: forecast_kernel(regions, band_rows, *refs),...  1.5 us
    pallas_call x1, Pallas kernels, local_direct(): pl.pallas_call(pack_kernel, out_shape=jax.ShapeDtypeStruct((fields * rows...  0.88 us
  transfers between devices with their start and end apart: 11, of which 4 were waited for; matrix products, arithmetic and copies ran while one was open for 0% of the time, Pallas kernels for 0%

profile of v3, /device:TPU:0, one launch (start us, length us, event | category | flops | bytes accessed | tf_op | source)
XLA Modules:
  0.0 20.6 jit_solution(6427342861941057667)
XLA Ops:
  0.0 0.9 %shard_map.46 = f32[52,128]{1,0:T(8,128)S(1)} custom-call(f32[48,128]{1,0:T(8,128)} %bitcast.2, s32[1,128]{1,0:T(1,128)} %cell_hbm.1, f32[1,128]{1,0:T(1,128)} %value_hbm.1, s32[1,128]{1,0:T(1,128)} %bin_hbm.1), custom_call_target="tpu_custom_call" | custom-call | tf_op jit(solution)/shard_map/pallas_call | solution.py:466
  0.9 2.5 %collective-permute-start.3 = (f32[52,128]{1,0:T(8,128)S(1)}, f32[52,128]{1,0:T(8,128)S(1)}, u32[]{:S(2)}, u32[]{:S(2)}) collective-permute-start(f32[52,128]{1,0:T(8,128)S(1)} %shard_map.46), channel_id=1, source_target_pairs={{7,0},{4,1},{5,2},{6,3},{3,4},{0,5},{1,6},{2,7},{15,8},{12,9},{13,... | collective-permute-start | bytes 79880 | tf_op jit(solution)/shard_map/ppermute | solution.py:490
  3.4 2.9 %collective-permute-start.2 = (f32[52,128]{1,0:T(8,128)S(1)}, f32[52,128]{1,0:T(8,128)S(1)}, u32[]{:S(2)}, u32[]{:S(2)}) collective-permute-start(f32[52,128]{1,0:T(8,128)S(1)} %shard_map.46), channel_id=1, source_target_pairs={{6,0},{7,1},{4,2},{5,3},{2,4},{3,5},{0,6},{1,7},{14,8},{15,9},{12,... | collective-permute-start | bytes 79880 | tf_op jit(solution)/shard_map/ppermute | solution.py:490
  6.3 0.8 %collective-permute-start.1 = (f32[52,128]{1,0:T(8,128)S(1)}, f32[52,128]{1,0:T(8,128)S(1)}, u32[]{:S(2)}, u32[]{:S(2)}) collective-permute-start(f32[52,128]{1,0:T(8,128)S(1)} %shard_map.46), channel_id=1, source_target_pairs={{5,0},{6,1},{7,2},{4,3},{1,4},{2,5},{3,6},{0,7},{13,8},{14,9},{15,... | collective-permute-start | bytes 79880 | tf_op jit(solution)/shard_map/ppermute | solution.py:490
  7.1 0.7 %collective-permute-start = (f32[52,128]{1,0:T(8,128)S(1)}, f32[52,128]{1,0:T(8,128)S(1)}, u32[]{:S(2)}, u32[]{:S(2)}) collective-permute-start(f32[52,128]{1,0:T(8,128)S(1)} %shard_map.46), channel_id=1, source_target_pairs={{4,0},{5,1},{6,2},{7,3},{0,4},{1,5},{2,6},{3,7},{12,8},{13,9},{14,... | collective-permute-start | bytes 79880 | tf_op jit(solution)/shard_map/ppermute | solution.py:490
  7.7 0.0 collective-permute-done.3.refs_3_
  7.7 0.4 %collective-permute-done.2.refs_2_ = f32[52,128]{1,0:T(8,128)S(1)} collective-permute-done((f32[52,128]{1,0:T(8,128)S(1)}, f32[52,128]{1,0:T(8,128)S(1)}, u32[]{:S(2)}, u32[]{:S(2)}) %collective-permute-start.2) | collective-permute-done | bytes 26656 | tf_op jit(solution)/shard_map/ppermute | solution.py:490
  8.1 1.7 %collective-permute-done.1.refs_1_ = f32[52,128]{1,0:T(8,128)S(1)} collective-permute-done((f32[52,128]{1,0:T(8,128)S(1)}, f32[52,128]{1,0:T(8,128)S(1)}, u32[]{:S(2)}, u32[]{:S(2)}) %collective-permute-start.1) | collective-permute-done | bytes 26656 | tf_op jit(solution)/shard_map/ppermute | solution.py:490
  9.9 0.0 collective-permute-done.refs_0_
  9.9 1.5 %shard_map.47.refs_1_ = f32[112,128]{1,0:T(8,128)S(1)} custom-call(f32[52,128]{1,0:T(8,128)S(1)} %collective-permute-done.refs_0_, f32[52,128]{1,0:T(8,128)S(1)} %collective-permute-done.1.refs_1_, f32[52,128]{1,0:T(8,128)S(1)} %collective-permute-done.2.refs_2_, f32[52,128]{1,0:T(8,128)S(1)} %collective-permute-done.3.refs_3_), custom_call_target="tpu_custom_call" | custom-call | tf_op jit(solution)/shard_map/pallas_call | solution.py:503
  11.4 2.2 %collective-permute-start.9 = (f32[112,128]{1,0:T(8,128)S(1)}, f32[112,128]{1,0:T(8,128)S(1)}, u32[]{:S(2)}, u32[]{:S(2)}) collective-permute-start(f32[112,128]{1,0:T(8,128)S(1)} %shard_map.47.refs_1_), channel_id=1, source_target_pairs={{0,28},{4,24},{8,20},{12,16},{16,12},{20,8},{24,4},{28,0},{1,29},{... | collective-permute-start | bytes 172040 | tf_op jit(solution)/shard_map/ppermute | solution.py:512
  13.6 0.5 %collective-permute-start.7 = (f32[112,128]{1,0:T(8,128)S(1)}, f32[112,128]{1,0:T(8,128)S(1)}, u32[]{:S(2)}, u32[]{:S(2)}) collective-permute-start(f32[112,128]{1,0:T(8,128)S(1)} %shard_map.47.refs_1_), channel_id=1, source_target_pairs={{0,20},{4,16},{8,28},{12,24},{16,4},{20,0},{24,12},{28,8},{1,21},{... | collective-permute-start | bytes 172040 | tf_op jit(solution)/shard_map/ppermute | solution.py:512
  14.1 0.5 %collective-permute-start.6 = (f32[112,128]{1,0:T(8,128)S(1)}, f32[112,128]{1,0:T(8,128)S(1)}, u32[]{:S(2)}, u32[]{:S(2)}) collective-permute-start(f32[112,128]{1,0:T(8,128)S(1)} %shard_map.47.refs_1_), channel_id=1, source_target_pairs={{0,8},{4,12},{8,0},{12,4},{16,24},{20,28},{24,16},{28,20},{1,9},{5... | collective-permute-start | bytes 172040 | tf_op jit(solution)/shard_map/ppermute | solution.py:512
  14.7 0.9 %collective-permute-start.5 = (f32[112,128]{1,0:T(8,128)S(1)}, f32[112,128]{1,0:T(8,128)S(1)}, u32[]{:S(2)}, u32[]{:S(2)}) collective-permute-start(f32[112,128]{1,0:T(8,128)S(1)} %shard_map.47.refs_1_), channel_id=1, source_target_pairs={{0,12},{4,8},{8,4},{12,0},{16,28},{20,24},{24,20},{28,16},{1,13},{... | collective-permute-start | bytes 172040 | tf_op jit(solution)/shard_map/ppermute | solution.py:512
  15.6 0.7 %collective-permute-start.4 = (f32[112,128]{1,0:T(8,128)S(1)}, f32[112,128]{1,0:T(8,128)S(1)}, u32[]{:S(2)}, u32[]{:S(2)}) collective-permute-start(f32[112,128]{1,0:T(8,128)S(1)} %shard_map.47.refs_1_), channel_id=1, source_target_pairs={{0,4},{4,0},{8,12},{12,8},{16,20},{20,16},{24,28},{28,24},{1,5},{5... | collective-permute-start | bytes 172040 | tf_op jit(solution)/shard_map/ppermute | solution.py:512
  16.3 0.0 collective-permute-done.9.refs_7_
  16.3 0.1 collective-permute-start.10
  16.4 0.9 %collective-permute-done.7.refs_5_ = f32[112,128]{1,0:T(8,128)S(1)} collective-permute-done((f32[112,128]{1,0:T(8,128)S(1)}, f32[112,128]{1,0:T(8,128)S(1)}, u32[]{:S(2)}, u32[]{:S(2)}) %collective-permute-start.7) | collective-permute-done | bytes 57376 | tf_op jit(solution)/shard_map/ppermute | solution.py:512
  17.3 0.7 %collective-permute-start.8 = (f32[112,128]{1,0:T(8,128)S(1)}, f32[112,128]{1,0:T(8,128)S(1)}, u32[]{:S(2)}, u32[]{:S(2)}) collective-permute-start(f32[112,128]{1,0:T(8,128)S(1)} %collective-permute-done.7.refs_5_), channel_id=1, source_target_pairs={{0,4},{4,0},{8,12},{12,8},{16,20},{20,16},{24,28},{28,24},{1,5},{5... | collective-permute-start | bytes 172040 | tf_op jit(solution)/shard_map/ppermute | solution.py:512
  17.9 1.0 %collective-permute-done.6.refs_4_ = f32[112,128]{1,0:T(8,128)S(1)} collective-permute-done((f32[112,128]{1,0:T(8,128)S(1)}, f32[112,128]{1,0:T(8,128)S(1)}, u32[]{:S(2)}, u32[]{:S(2)}) %collective-permute-start.6) | collective-permute-done | bytes 57376 | tf_op jit(solution)/shard_map/ppermute | solution.py:512
  18.9 0.0 collective-permute-done.5.refs_3_
  18.9 0.0 collective-permute-done.4.refs_2_
  18.9 0.0 collective-permute-done.10.refs_8_
  18.9 0.0 collective-permute-done.8.refs_6_
  18.9 1.6 %shard_map.48 = f32[1,3,16,128]{3,2,1,0:T(8,128)} custom-call(s32[1]{0:T(128)} %bitcast.refs_0_, f32[112,128]{1,0:T(8,128)S(1)} %shard_map.47.refs_1_, f32[112,128]{1,0:T(8,128)S(1)} %collective-permute-done.4.refs_2_, f32[112,128]{1,0:T(8,128)S(1)} %collective-permute-done.5.refs_3_, f32[112,128]{1,0:T(8,128)S(1)} %collective-permute-done.6.refs_4_, ...), custom_call_target="tpu_custom_call" | custom-call | tf_op jit(solution)/shard_map/pallas_call | solution.py:522
Async XLA Ops:
  0.9 6.9 %collective-permute-start.3 = (f32[52,128]{1,0:T(8,128)S(1)}, f32[52,128]{1,0:T(8,128)S(1)}, u32[]{:S(2)}, u32[]{:S(2)}) collective-permute-start(f32[52,128]{1,0:T(8,128)S(1)} %shard_map.46), channel_id=1, source_target_pairs={{7,0},{4,1},{5,2},{6,3},{3,4},{0,5},{1,6},{2,7},{15,8},{12,9},{13,... | collective-permute-start | bytes 79880 | tf_op jit(solution)/shard_map/ppermute | solution.py:490
  3.4 4.7 %collective-permute-start.2 = (f32[52,128]{1,0:T(8,128)S(1)}, f32[52,128]{1,0:T(8,128)S(1)}, u32[]{:S(2)}, u32[]{:S(2)}) collective-permute-start(f32[52,128]{1,0:T(8,128)S(1)} %shard_map.46), channel_id=1, source_target_pairs={{6,0},{7,1},{4,2},{5,3},{2,4},{3,5},{0,6},{1,7},{14,8},{15,9},{12,... | collective-permute-start | bytes 79880 | tf_op jit(solution)/shard_map/ppermute | solution.py:490
  6.3 3.6 %collective-permute-start.1 = (f32[52,128]{1,0:T(8,128)S(1)}, f32[52,128]{1,0:T(8,128)S(1)}, u32[]{:S(2)}, u32[]{:S(2)}) collective-permute-start(f32[52,128]{1,0:T(8,128)S(1)} %shard_map.46), channel_id=1, source_target_pairs={{5,0},{6,1},{7,2},{4,3},{1,4},{2,5},{3,6},{0,7},{13,8},{14,9},{15,... | collective-permute-start | bytes 79880 | tf_op jit(solution)/shard_map/ppermute | solution.py:490
  7.1 2.8 %collective-permute-start = (f32[52,128]{1,0:T(8,128)S(1)}, f32[52,128]{1,0:T(8,128)S(1)}, u32[]{:S(2)}, u32[]{:S(2)}) collective-permute-start(f32[52,128]{1,0:T(8,128)S(1)} %shard_map.46), channel_id=1, source_target_pairs={{4,0},{5,1},{6,2},{7,3},{0,4},{1,5},{2,6},{3,7},{12,8},{13,9},{14,... | collective-permute-start | bytes 79880 | tf_op jit(solution)/shard_map/ppermute | solution.py:490
  11.4 4.9 %collective-permute-start.9 = (f32[112,128]{1,0:T(8,128)S(1)}, f32[112,128]{1,0:T(8,128)S(1)}, u32[]{:S(2)}, u32[]{:S(2)}) collective-permute-start(f32[112,128]{1,0:T(8,128)S(1)} %shard_map.47.refs_1_), channel_id=1, source_target_pairs={{0,28},{4,24},{8,20},{12,16},{16,12},{20,8},{24,4},{28,0},{1,29},{... | collective-permute-start | bytes 172040 | tf_op jit(solution)/shard_map/ppermute | solution.py:512
  13.6 3.7 %collective-permute-start.7 = (f32[112,128]{1,0:T(8,128)S(1)}, f32[112,128]{1,0:T(8,128)S(1)}, u32[]{:S(2)}, u32[]{:S(2)}) collective-permute-start(f32[112,128]{1,0:T(8,128)S(1)} %shard_map.47.refs_1_), channel_id=1, source_target_pairs={{0,20},{4,16},{8,28},{12,24},{16,4},{20,0},{24,12},{28,8},{1,21},{... | collective-permute-start | bytes 172040 | tf_op jit(solution)/shard_map/ppermute | solution.py:512
  14.1 4.8 %collective-permute-start.6 = (f32[112,128]{1,0:T(8,128)S(1)}, f32[112,128]{1,0:T(8,128)S(1)}, u32[]{:S(2)}, u32[]{:S(2)}) collective-permute-start(f32[112,128]{1,0:T(8,128)S(1)} %shard_map.47.refs_1_), channel_id=1, source_target_pairs={{0,8},{4,12},{8,0},{12,4},{16,24},{20,28},{24,16},{28,20},{1,9},{5... | collective-permute-start | bytes 172040 | tf_op jit(solution)/shard_map/ppermute | solution.py:512
  14.7 4.2 %collective-permute-start.5 = (f32[112,128]{1,0:T(8,128)S(1)}, f32[112,128]{1,0:T(8,128)S(1)}, u32[]{:S(2)}, u32[]{:S(2)}) collective-permute-start(f32[112,128]{1,0:T(8,128)S(1)} %shard_map.47.refs_1_), channel_id=1, source_target_pairs={{0,12},{4,8},{8,4},{12,0},{16,28},{20,24},{24,20},{28,16},{1,13},{... | collective-permute-start | bytes 172040 | tf_op jit(solution)/shard_map/ppermute | solution.py:512
  15.6 3.3 %collective-permute-start.4 = (f32[112,128]{1,0:T(8,128)S(1)}, f32[112,128]{1,0:T(8,128)S(1)}, u32[]{:S(2)}, u32[]{:S(2)}) collective-permute-start(f32[112,128]{1,0:T(8,128)S(1)} %shard_map.47.refs_1_), channel_id=1, source_target_pairs={{0,4},{4,0},{8,12},{12,8},{16,20},{20,16},{24,28},{28,24},{1,5},{5... | collective-permute-start | bytes 172040 | tf_op jit(solution)/shard_map/ppermute | solution.py:512
  16.3 2.6 %collective-permute-start.10 = (f32[112,128]{1,0:T(8,128)S(1)}, f32[112,128]{1,0:T(8,128)S(1)}, u32[]{:S(2)}, u32[]{:S(2)}) collective-permute-start(f32[112,128]{1,0:T(8,128)S(1)} %collective-permute-done.9.refs_7_), channel_id=1, source_target_pairs={{0,4},{4,0},{8,12},{12,8},{16,20},{20,16},{24,28},{28,24},{1,5},{5... | collective-permute-start | bytes 172040 | tf_op jit(solution)/shard_map/ppermute | solution.py:512
  17.3 1.6 %collective-permute-start.8 = (f32[112,128]{1,0:T(8,128)S(1)}, f32[112,128]{1,0:T(8,128)S(1)}, u32[]{:S(2)}, u32[]{:S(2)}) collective-permute-start(f32[112,128]{1,0:T(8,128)S(1)} %collective-permute-done.7.refs_5_), channel_id=1, source_target_pairs={{0,4},{4,0},{8,12},{12,8},{16,20},{20,16},{24,28},{28,24},{1,5},{5... | collective-permute-start | bytes 172040 | tf_op jit(solution)/shard_map/ppermute | solution.py:512

commit v4 on v3

--- a/solution.py
+++ b/solution.py
@@ -191,10 +191,24 @@
     )
 
 
-def pack_kernel(prior_hbm, cell_hbm, value_hbm, bin_hbm, pack_ref, cell_ref, value_ref, bin_ref, sems):
+def by_class(lane, columns, slabs):
+    width = columns // slabs
+    return slabs * (lane % width) + lane // width
+
+
+def own_part(parts, lane):
+    slabs = len(parts)
+    result = None
+    for w, part in enumerate(parts):
+        taken = jnp.take_along_axis(part, lane // slabs, axis=1)
+        result = taken if w == 0 else jnp.where(lane % slabs == w, taken, result)
+    return result
+
+
+def pack_kernel(slabs, prior_hbm, cell_hbm, value_hbm, bin_hbm, pack_ref, prior_ref, cell_ref, value_ref, bin_ref, sems):
     taken, columns = prior_hbm.shape
     count = cell_hbm.shape[1]
-    prior_copy = pltpu.make_async_copy(prior_hbm, pack_ref.at[pl.ds(0, taken), :], sems.at[0])
+    prior_copy = pltpu.make_async_copy(prior_hbm, prior_ref, sems.at[0])
     copies = [
         pltpu.make_async_copy(source, target, sems.at[1 + i])
         for i, (source, target) in enumerate(
@@ -214,7 +228,8 @@
         rest = rest - part
     parts.append(jnp.zeros((2, count), jnp.float32))
     total = (pack_ref.shape[0] - taken) // 2 * columns
-    at_cell = lax.broadcasted_iota(jnp.int32, (total, count), 0) == cell_ref[...]
+    at = lax.broadcasted_iota(jnp.int32, (total, count), 0)
+    at_cell = at // columns * columns + by_class(at % columns, columns, slabs) == cell_ref[...]
     sums = lax.dot_general(
         jnp.concatenate(parts, axis=0).astype(jnp.bfloat16),
         jnp.where(at_cell, 1.0, 0.0).astype(jnp.bfloat16),
@@ -225,7 +240,10 @@
     for row in range(total // columns):
         part = slice(row * columns, (row + 1) * columns)
         pack_ref[taken + 2 * row : taken + 2 * row + 2, :] = sums[:, part]
+    place = by_class(lax.broadcasted_iota(jnp.int32, (8, columns), 1), columns, slabs)
     prior_copy.wait()
+    for row in range(0, taken, 8):
+        pack_ref[row : row + 8, :] = jnp.take_along_axis(prior_ref[row : row + 8, :], place, axis=1)
 
 
 def forecast_kernel(regions, band_rows, *refs):
@@ -233,31 +251,42 @@
     slabs = len(pack_refs)
     rows = regions * band_rows
     columns = out_ref.shape[1]
-    width = slabs * columns
+    width = columns // slabs
+
+    def interleaved(parts):
+        block = lax.broadcasted_iota(jnp.int32, parts[0].shape, 1) // width
+
+        def chosen(pick):
+            result = pick(0)
+            for k in range(1, slabs):
+                result = jnp.where(block == k, pick(k), result)
+            return result
+
+        turned = []
+        for d in range(slabs):
+            mixed = chosen(lambda k: parts[(k + d) % slabs])
+            turned.append(pltpu.roll(mixed, d * width, 1) if d else mixed)
+        return [chosen(lambda p: turned[(p - w) % slabs]) for w in range(slabs)]
 
     def field_of(field):
         return [
-            jnp.concatenate(
-                [ref[pl.ds(field * rows + q, regions, stride=band_rows), :] for ref in pack_refs],
-                axis=1,
+            interleaved(
+                [ref[pl.ds(field * rows + q, regions, stride=band_rows), :] for ref in pack_refs]
             )
             for q in range(band_rows)
         ]
 
-    def east(x):
-        return [
-            x[q + 1] if q + 1 < band_rows else pltpu.roll(x[0], regions - 1, 0)
-            for q in range(band_rows)
-        ]
-
-    def west(x):
-        return [x[q - 1] if q > 0 else pltpu.roll(x[-1], 1, 0) for q in range(band_rows)]
-
-    def north(x):
-        return [pltpu.roll(part, width - 1, 1) for part in x]
-
-    def south(x):
-        return [pltpu.roll(part, 1, 1) for part in x]
+    def east(x, q, w):
+        return x[q + 1][w] if q + 1 < band_rows else pltpu.roll(x[0][w], regions - 1, 0)
+
+    def west(x, q, w):
+        return x[q - 1][w] if q > 0 else pltpu.roll(x[-1][w], 1, 0)
+
+    def north(x, q, w):
+        return x[q][w + 1] if w + 1 < slabs else pltpu.roll(x[q][0], columns - 1, 1)
+
+    def south(x, q, w):
+        return x[q][w - 1] if w > 0 else pltpu.roll(x[q][-1], 1, 1)
 
     keep = 1.0 - 4.0 * time_step * viscosity
     blend = time_step * viscosity
@@ -266,30 +295,33 @@
 
     def step(counter, state):
         h, u, v = state
-        he, hw, hn, hs = east(h), west(h), north(h), south(h)
-        ue, uw, un, us = east(u), west(u), north(u), south(u)
-        ve, vw, vn, vs = east(v), west(v), north(v), south(v)
         new_h, new_u, new_v = [], [], []
         for q in range(band_rows):
-            ux, uy = ue[q] - uw[q], un[q] - us[q]
-            vx, vy = ve[q] - vw[q], vn[q] - vs[q]
-            flux_x = mean_depth * ux + (he[q] * ue[q] - hw[q] * uw[q])
-            flux_y = mean_depth * vy + (hn[q] * vn[q] - hs[q] * vs[q])
-            new_h.append(
-                keep * h[q]
-                + blend * ((he[q] + hw[q]) + (hn[q] + hs[q]))
-                - half * (flux_x + flux_y)
-            )
-            new_u.append(
-                (keep * u[q] + turn * v[q])
-                + blend * ((ue[q] + uw[q]) + (un[q] + us[q]))
-                - half * ((u[q] * ux + v[q] * uy) + gravity * (he[q] - hw[q]))
-            )
-            new_v.append(
-                (keep * v[q] - turn * u[q])
-                + blend * ((ve[q] + vw[q]) + (vn[q] + vs[q]))
-                - half * ((u[q] * vx + v[q] * vy) + gravity * (hn[q] - hs[q]))
-            )
+            for row in (new_h, new_u, new_v):
+                row.append([])
+            for w in range(slabs):
+                sides = [
+                    [side(x, q, w) for side in (east, west, north, south)] for x in (h, u, v)
+                ]
+                (he, hw, hn, hs), (ue, uw, un, us), (ve, vw, vn, vs) = sides
+                hm, um, vm = h[q][w], u[q][w], v[q][w]
+                ux, uy = ue - uw, un - us
+                vx, vy = ve - vw, vn - vs
+                flux_x = mean_depth * ux + (he * ue - hw * uw)
+                flux_y = mean_depth * vy + (hn * vn - hs * vs)
+                new_h[q].append(
+                    keep * hm + blend * ((he + hw) + (hn + hs)) - half * (flux_x + flux_y)
+                )
+                new_u[q].append(
+                    (keep * um + turn * vm)
+                    + blend * ((ue + uw) + (un + us))
+                    - half * ((um * ux + vm * uy) + gravity * (he - hw))
+                )
+                new_v[q].append(
+                    (keep * vm - turn * um)
+                    + blend * ((ve + vw) + (vn + vs))
+                    - half * ((um * vx + vm * vy) + gravity * (hn - hs))
+                )
         return new_h, new_u, new_v
 
     h, u, v = lax.fori_loop(
@@ -297,23 +329,26 @@
     )
     at = 0
     for q in range(band_rows):
-        for slab in range(slabs):
-            out_ref[at : at + regions, :] = h[q][:, slab * columns : (slab + 1) * columns]
+        for w in range(slabs):
+            out_ref[at : at + regions, :] = h[q][w]
             at += regions
+    lane = lax.broadcasted_iota(jnp.int32, (regions, columns), 1)
     for field in (u, v):
         for q in range(band_rows):
-            out_ref[at : at + regions, :] = field[q][:, :columns]
+            out_ref[at : at + regions, :] = own_part(field[q], lane)
             at += regions
+    base = 3 * rows
+    sums = interleaved([ref[base : base + 2 * band_rows, :] for ref in pack_refs])
     for q in range(band_rows):
-        for ref in pack_refs:
-            base = 3 * rows + 2 * q
-            out_ref[at : at + 2, :] = ref[base : base + 2, :]
+        for w in range(slabs):
+            out_ref[at : at + 2, :] = sums[w][2 * q : 2 * q + 2, :]
             at += 2
 
 
 def analysis_kernel(order, band_rows, slabs, me_ref, *refs):
     members = regions = len(order)
-    pack_refs, out_ref, sums_ref = [refs[order.index(b)] for b in range(members)], refs[-2], refs[-1]
+    pack_refs = [refs[order.index(b)] for b in range(members)]
+    out_ref, sums_ref, rows_ref = refs[-3:]
     columns = out_ref.shape[3]
     tall = regions
     h_rows = band_rows * slabs * tall
@@ -376,62 +411,68 @@
     on_diagonal = (flat_lane < members * members) & (flat_lane % (members + 1) == 0)
     stacked = jnp.where(on_diagonal, stacked + (members - 1) / inflation, stacked)
 
-    turned = jnp.transpose(
-        jnp.concatenate(
-            [stacked, jnp.zeros((128 - stacked.shape[0], 128), jnp.float32)], axis=0
-        )
-    )
+    turned = jnp.transpose(stacked)
+    wide = turned.shape[1]
     gram = [turned[i * members : (i + 1) * members, :] for i in range(members)]
     pull = turned[members * members : members * members + members, :]
-    sub = lax.broadcasted_iota(jnp.int32, (members, 128), 0)
+    sub = lax.broadcasted_iota(jnp.int32, (members, wide), 0)
 
     trace = None
     for i in range(members):
         part = gram[i][i : i + 1, :]
         trace = part if trace is None else trace + part
-    live = lax.broadcasted_iota(jnp.int32, (1, 128), 1) < stacked.shape[0]
-    trace = jnp.where(live, trace, 1.0)
     eye = [jnp.where(sub == i, 1.0, 0.0) for i in range(members)]
 
     def across(row):
-        return jnp.broadcast_to(row, (members, 128))
-
-    def product(left, right):
+        return jnp.broadcast_to(row, (members, wide))
+
+    taken = [0]
+
+    def spread_rows(parts):
+        base = taken[0]
+        taken[0] += len(parts) * members
+        for i, part in enumerate(parts):
+            rows_ref[base + i * members : base + (i + 1) * members, :] = part
+        return [
+            [
+                across(rows_ref[base + i * members + k : base + i * members + k + 1, :])
+                for k in range(members)
+            ]
+            for i in range(len(parts))
+        ]
+
+    def product(left_rows, right):
         result = []
-        for i in range(members):
-            terms = [across(left[i][k : k + 1, :]) * right[k] for k in range(members)]
+        for i in range(len(left_rows)):
+            terms = [left_rows[i][k] * right[k] for k in range(members)]
             while len(terms) > 1:
                 terms = [x + y for x, y in zip(terms[::2], terms[1::2])]
             result.append(terms[0])
         return result
 
     def applied(matrix, vector):
-        terms = [across(vector[k : k + 1, :]) * matrix[k] for k in range(members)]
-        while len(terms) > 1:
-            terms = [x + y for x, y in zip(terms[::2], terms[1::2])]
-        return terms[0]
+        return product(spread_rows([vector]), matrix)[0]
 
     scale = 1.0 / trace
-    y = [part * across(scale) for part in gram]
-    z = None
+    own = eye[beside] * across(lax.rsqrt(trace))
+    mean_weight = pull * across(scale)
+    e = [one - part * across(scale) for one, part in zip(eye, gram)]
     for sweep in range(SWEEPS):
-        zy = y if z is None else product(z, y)
-        k = [1.5 * e - 0.5 * part for e, part in zip(eye, zy)]
-        if sweep < SWEEPS - 1:
-            y = product(y, k)
-            z = k if z is None else product(k, z)
-
-    def rooted(vector):
-        return applied(k, applied(z, vector))
-
-    root_scale = lax.rsqrt(trace)
-    mean_weight = rooted(rooted(pull)) * across(scale)
-    own = rooted(eye[beside]) * across(root_scale)
+        k = [one + 0.5 * part for one, part in zip(eye, e)]
+        own = applied(k, own)
+        if sweep == SWEEPS - 1:
+            mean_weight = applied(k, applied(k, mean_weight))
+        else:
+            square = product(spread_rows(e), e)
+            twice = [one + part + 0.25 * more for one, part, more in zip(eye, e, square)]
+            mean_weight = applied(twice, mean_weight)
+            e = product(
+                spread_rows(square), [0.75 * one + 0.25 * part for one, part in zip(eye, e)]
+            )
     mixing = math.sqrt(members - 1) * own + mean_weight
 
-    back = jnp.transpose(
-        jnp.concatenate([mixing, jnp.zeros((128 - members, 128), jnp.float32)], axis=0)
-    )
+    back = jnp.transpose(mixing)
+    place = lax.broadcasted_iota(jnp.int32, (regions, columns), 1)
     for t in range(band_rows):
         part = back[t * regions : (t + 1) * regions, :]
         share = [
@@ -439,14 +480,18 @@
         ]
         for field in range(3):
             if field == 0:
-                at = t * slabs * tall
+                starts = [(t * slabs + w) * tall for w in range(slabs)]
             else:
-                at = h_rows + ((field - 1) * band_rows + t) * tall
-            values = [ref[at : at + tall, :] for ref in pack_refs]
-            mean = sum(values[1:], values[0]) * (1.0 / members)
-            result = mean
-            for m in range(members):
-                result = result + (values[m] - mean) * share[m]
+                starts = [h_rows + ((field - 1) * band_rows + t) * tall]
+            results = []
+            for at in starts:
+                values = [ref[at : at + tall, :] for ref in pack_refs]
+                mean = sum(values[1:], values[0]) * (1.0 / members)
+                result = mean
+                for m in range(members):
+                    result = result + (values[m] - mean) * share[m]
+                results.append(result)
+            result = own_part(results, place) if field == 0 else results[0]
             out_ref[0, field, pl.ds(t, regions, stride=band_rows), :] = result
 
 
@@ -464,11 +509,12 @@
     regions = members
     band_rows = rows // regions
     pack = pl.pallas_call(
-        pack_kernel,
+        lambda *refs: pack_kernel(slabs, *refs),
         out_shape=jax.ShapeDtypeStruct((fields * rows + 2 * band_rows, columns), jnp.float32),
         in_specs=[pl.BlockSpec(memory_space=pltpu.HBM)] * 4,
         out_specs=pl.BlockSpec(memory_space=pltpu.VMEM),
         scratch_shapes=[
+            pltpu.VMEM((fields * rows, columns), jnp.float32),
             pltpu.VMEM(obs_cell.shape, obs_cell.dtype),
             pltpu.VMEM(obs_value.shape, obs_value.dtype),
             pltpu.VMEM(obs_bin.shape, obs_bin.dtype),
@@ -527,6 +573,7 @@
         compiler_params=small_grant,
         scratch_shapes=[
             pltpu.VMEM((regions * 2 * band_rows * slabs, columns), jnp.float32),
+            pltpu.VMEM((2 * SWEEPS * members * (members + 2), rows), jnp.float32),
         ],
     )(me, *[blocks[b] for b in order])
 
@@ -538,7 +585,8 @@
         _, fields, rows, columns = prior_sample_stack.shape
         power = members & (members - 1) == 0
         small = members * (members + 1) <= 128 and rows <= 128 and members % 8 == 0
-        if power and small and columns == 128 and rows % members == 0:
+        fits = columns == 128 and columns % slabs == 0 and rows % members == 0
+        if power and small and fits:
             return local_direct(prior_sample_stack, obs_cell, obs_value, obs_bin)
         return local_general(prior_sample_stack, obs_cell, obs_value, obs_bin)
 

time: 20.7 us -> 20.3 us (0.981)
  Pallas kernels: 4.02 us -> 3.63 us
    pallas_call x1, Pallas kernels: 1.5 us -> 1.1 us  [local_direct(): pl.pallas_call(lambda *refs: forecast_kernel(regions, band_rows, *refs),...]
where the time goes in v4:
time: 20.3 us; the launch traced here: 20.1 us
  starting transfers between devices  12.5 us (62%)
  waiting for transfers between devices  3.99 us (20%)
  Pallas kernels  3.63 us (18%)
    ppermute x4, starting transfers between devices, local_direct(): lax.ppermute(pack, ('mem', 'slab'), [((m ^ beside) * slabs + (s + ahead)...  6.85 us
    ppermute x7, starting transfers between devices, partner(): return lax.ppermute(value, 'mem', [(i, i ^ bits) for i in range(members)])  5.62 us
    ppermute x4, waiting for transfers between devices, local_direct(): lax.ppermute(pack, ('mem', 'slab'), [((m ^ beside) * slabs + (s + ahead)...  2.12 us
    ppermute x7, waiting for transfers between devices, partner(): return lax.ppermute(value, 'mem', [(i, i ^ bits) for i in range(members)])  1.87 us
    pallas_call x1, Pallas kernels, local_direct(): pl.pallas_call(lambda *refs: analysis_kernel(order, band_rows, slabs, *re...  1.54 us
    pallas_call x1, Pallas kernels, local_direct(): pl.pallas_call(lambda *refs: forecast_kernel(regions, band_rows, *refs),...  1.1 us
    pallas_call x1, Pallas kernels, local_direct(): pl.pallas_call(lambda *refs: pack_kernel(slabs, *refs), out_shape=jax.Sha...  0.98 us
  transfers between devices with their start and end apart: 11, of which 4 were waited for; matrix products, arithmetic and copies ran while one was open for 0% of the time, Pallas kernels for 0%

profile of v4, /device:TPU:0, one launch (start us, length us, event | category | flops | bytes accessed | tf_op | source)
XLA Modules:
  0.0 20.1 jit_solution(1500308378955449441)
XLA Ops:
  0.0 1.0 %shard_map.46 = f32[52,128]{1,0:T(8,128)S(1)} custom-call(f32[48,128]{1,0:T(8,128)} %bitcast.2, s32[1,128]{1,0:T(1,128)} %refs_1_.1, f32[1,128]{1,0:T(1,128)} %refs_2_.1, s32[1,128]{1,0:T(1,128)} %refs_3_.1), custom_call_target="tpu_custom_call" | custom-call | tf_op jit(solution)/shard_map/pallas_call | solution.py:511
  1.0 2.5 %collective-permute-start.3 = (f32[52,128]{1,0:T(8,128)S(1)}, f32[52,128]{1,0:T(8,128)S(1)}, u32[]{:S(2)}, u32[]{:S(2)}) collective-permute-start(f32[52,128]{1,0:T(8,128)S(1)} %shard_map.46), channel_id=1, source_target_pairs={{7,0},{4,1},{5,2},{6,3},{3,4},{0,5},{1,6},{2,7},{15,8},{12,9},{13,... | collective-permute-start | bytes 79880 | tf_op jit(solution)/shard_map/ppermute | solution.py:536
  3.5 2.9 %collective-permute-start.2 = (f32[52,128]{1,0:T(8,128)S(1)}, f32[52,128]{1,0:T(8,128)S(1)}, u32[]{:S(2)}, u32[]{:S(2)}) collective-permute-start(f32[52,128]{1,0:T(8,128)S(1)} %shard_map.46), channel_id=1, source_target_pairs={{6,0},{7,1},{4,2},{5,3},{2,4},{3,5},{0,6},{1,7},{14,8},{15,9},{12,... | collective-permute-start | bytes 79880 | tf_op jit(solution)/shard_map/ppermute | solution.py:536
  6.4 0.8 %collective-permute-start.1 = (f32[52,128]{1,0:T(8,128)S(1)}, f32[52,128]{1,0:T(8,128)S(1)}, u32[]{:S(2)}, u32[]{:S(2)}) collective-permute-start(f32[52,128]{1,0:T(8,128)S(1)} %shard_map.46), channel_id=1, source_target_pairs={{5,0},{6,1},{7,2},{4,3},{1,4},{2,5},{3,6},{0,7},{13,8},{14,9},{15,... | collective-permute-start | bytes 79880 | tf_op jit(solution)/shard_map/ppermute | solution.py:536
  7.2 0.7 %collective-permute-start = (f32[52,128]{1,0:T(8,128)S(1)}, f32[52,128]{1,0:T(8,128)S(1)}, u32[]{:S(2)}, u32[]{:S(2)}) collective-permute-start(f32[52,128]{1,0:T(8,128)S(1)} %shard_map.46), channel_id=1, source_target_pairs={{4,0},{5,1},{6,2},{7,3},{0,4},{1,5},{2,6},{3,7},{12,8},{13,9},{14,... | collective-permute-start | bytes 79880 | tf_op jit(solution)/shard_map/ppermute | solution.py:536
  7.8 0.0 collective-permute-done.3.refs_3_
  7.8 0.4 %collective-permute-done.2.refs_2_ = f32[52,128]{1,0:T(8,128)S(1)} collective-permute-done((f32[52,128]{1,0:T(8,128)S(1)}, f32[52,128]{1,0:T(8,128)S(1)}, u32[]{:S(2)}, u32[]{:S(2)}) %collective-permute-start.2) | collective-permute-done | bytes 26656 | tf_op jit(solution)/shard_map/ppermute | solution.py:536
  8.2 1.7 %collective-permute-done.1.refs_1_ = f32[52,128]{1,0:T(8,128)S(1)} collective-permute-done((f32[52,128]{1,0:T(8,128)S(1)}, f32[52,128]{1,0:T(8,128)S(1)}, u32[]{:S(2)}, u32[]{:S(2)}) %collective-permute-start.1) | collective-permute-done | bytes 26656 | tf_op jit(solution)/shard_map/ppermute | solution.py:536
  10.0 0.0 collective-permute-done.refs_0_
  10.0 1.1 %shard_map.47.refs_1_ = f32[112,128]{1,0:T(8,128)S(1)} custom-call(f32[52,128]{1,0:T(8,128)S(1)} %collective-permute-done.refs_0_, f32[52,128]{1,0:T(8,128)S(1)} %collective-permute-done.1.refs_1_, f32[52,128]{1,0:T(8,128)S(1)} %collective-permute-done.2.refs_2_, f32[52,128]{1,0:T(8,128)S(1)} %collective-permute-done.3.refs_3_), custom_call_target="tpu_custom_call" | custom-call | tf_op jit(solution)/shard_map/pallas_call | solution.py:549
  11.1 2.2 %collective-permute-start.9 = (f32[112,128]{1,0:T(8,128)S(1)}, f32[112,128]{1,0:T(8,128)S(1)}, u32[]{:S(2)}, u32[]{:S(2)}) collective-permute-start(f32[112,128]{1,0:T(8,128)S(1)} %shard_map.47.refs_1_), channel_id=1, source_target_pairs={{0,28},{4,24},{8,20},{12,16},{16,12},{20,8},{24,4},{28,0},{1,29},{... | collective-permute-start | bytes 172040 | tf_op jit(solution)/shard_map/ppermute | solution.py:558
  13.3 0.5 %collective-permute-start.7 = (f32[112,128]{1,0:T(8,128)S(1)}, f32[112,128]{1,0:T(8,128)S(1)}, u32[]{:S(2)}, u32[]{:S(2)}) collective-permute-start(f32[112,128]{1,0:T(8,128)S(1)} %shard_map.47.refs_1_), channel_id=1, source_target_pairs={{0,20},{4,16},{8,28},{12,24},{16,4},{20,0},{24,12},{28,8},{1,21},{... | collective-permute-start | bytes 172040 | tf_op jit(solution)/shard_map/ppermute | solution.py:558
  13.8 0.5 %collective-permute-start.6 = (f32[112,128]{1,0:T(8,128)S(1)}, f32[112,128]{1,0:T(8,128)S(1)}, u32[]{:S(2)}, u32[]{:S(2)}) collective-permute-start(f32[112,128]{1,0:T(8,128)S(1)} %shard_map.47.refs_1_), channel_id=1, source_target_pairs={{0,8},{4,12},{8,0},{12,4},{16,24},{20,28},{24,16},{28,20},{1,9},{5... | collective-permute-start | bytes 172040 | tf_op jit(solution)/shard_map/ppermute | solution.py:558
  14.3 0.9 %collective-permute-start.5 = (f32[112,128]{1,0:T(8,128)S(1)}, f32[112,128]{1,0:T(8,128)S(1)}, u32[]{:S(2)}, u32[]{:S(2)}) collective-permute-start(f32[112,128]{1,0:T(8,128)S(1)} %shard_map.47.refs_1_), channel_id=1, source_target_pairs={{0,12},{4,8},{8,4},{12,0},{16,28},{20,24},{24,20},{28,16},{1,13},{... | collective-permute-start | bytes 172040 | tf_op jit(solution)/shard_map/ppermute | solution.py:558
  15.2 0.7 %collective-permute-start.4 = (f32[112,128]{1,0:T(8,128)S(1)}, f32[112,128]{1,0:T(8,128)S(1)}, u32[]{:S(2)}, u32[]{:S(2)}) collective-permute-start(f32[112,128]{1,0:T(8,128)S(1)} %shard_map.47.refs_1_), channel_id=1, source_target_pairs={{0,4},{4,0},{8,12},{12,8},{16,20},{20,16},{24,28},{28,24},{1,5},{5... | collective-permute-start | bytes 172040 | tf_op jit(solution)/shard_map/ppermute | solution.py:558
  15.9 0.0 collective-permute-done.9.refs_7_
  15.9 0.1 collective-permute-start.10
  16.0 0.9 %collective-permute-done.7.refs_5_ = f32[112,128]{1,0:T(8,128)S(1)} collective-permute-done((f32[112,128]{1,0:T(8,128)S(1)}, f32[112,128]{1,0:T(8,128)S(1)}, u32[]{:S(2)}, u32[]{:S(2)}) %collective-permute-start.7) | collective-permute-done | bytes 57376 | tf_op jit(solution)/shard_map/ppermute | solution.py:558
  16.9 0.7 %collective-permute-start.8 = (f32[112,128]{1,0:T(8,128)S(1)}, f32[112,128]{1,0:T(8,128)S(1)}, u32[]{:S(2)}, u32[]{:S(2)}) collective-permute-start(f32[112,128]{1,0:T(8,128)S(1)} %collective-permute-done.7.refs_5_), channel_id=1, source_target_pairs={{0,4},{4,0},{8,12},{12,8},{16,20},{20,16},{24,28},{28,24},{1,5},{5... | collective-permute-start | bytes 172040 | tf_op jit(solution)/shard_map/ppermute | solution.py:558
  17.6 1.0 %collective-permute-done.6.refs_4_ = f32[112,128]{1,0:T(8,128)S(1)} collective-permute-done((f32[112,128]{1,0:T(8,128)S(1)}, f32[112,128]{1,0:T(8,128)S(1)}, u32[]{:S(2)}, u32[]{:S(2)}) %collective-permute-start.6) | collective-permute-done | bytes 57376 | tf_op jit(solution)/shard_map/ppermute | solution.py:558
  18.6 0.0 collective-permute-done.5.refs_3_
  18.6 0.0 collective-permute-done.4.refs_2_
  18.6 0.0 collective-permute-done.10.refs_8_
  18.6 0.0 collective-permute-done.8.refs_6_
  18.6 1.5 %shard_map.48 = f32[1,3,16,128]{3,2,1,0:T(8,128)} custom-call(s32[1]{0:T(128)} %bitcast.refs_0_, f32[112,128]{1,0:T(8,128)S(1)} %shard_map.47.refs_1_, f32[112,128]{1,0:T(8,128)S(1)} %collective-permute-done.4.refs_2_, f32[112,128]{1,0:T(8,128)S(1)} %collective-permute-done.5.refs_3_, f32[112,128]{1,0:T(8,128)S(1)} %collective-permute-done.6.refs_4_, ...), custom_call_target="tpu_custom_call" | custom-call | tf_op jit(solution)/shard_map/pallas_call | solution.py:568
Async XLA Ops:
  1.0 6.9 %collective-permute-start.3 = (f32[52,128]{1,0:T(8,128)S(1)}, f32[52,128]{1,0:T(8,128)S(1)}, u32[]{:S(2)}, u32[]{:S(2)}) collective-permute-start(f32[52,128]{1,0:T(8,128)S(1)} %shard_map.46), channel_id=1, source_target_pairs={{7,0},{4,1},{5,2},{6,3},{3,4},{0,5},{1,6},{2,7},{15,8},{12,9},{13,... | collective-permute-start | bytes 79880 | tf_op jit(solution)/shard_map/ppermute | solution.py:536
  3.5 4.7 %collective-permute-start.2 = (f32[52,128]{1,0:T(8,128)S(1)}, f32[52,128]{1,0:T(8,128)S(1)}, u32[]{:S(2)}, u32[]{:S(2)}) collective-permute-start(f32[52,128]{1,0:T(8,128)S(1)} %shard_map.46), channel_id=1, source_target_pairs={{6,0},{7,1},{4,2},{5,3},{2,4},{3,5},{0,6},{1,7},{14,8},{15,9},{12,... | collective-permute-start | bytes 79880 | tf_op jit(solution)/shard_map/ppermute | solution.py:536
  6.4 3.6 %collective-permute-start.1 = (f32[52,128]{1,0:T(8,128)S(1)}, f32[52,128]{1,0:T(8,128)S(1)}, u32[]{:S(2)}, u32[]{:S(2)}) collective-permute-start(f32[52,128]{1,0:T(8,128)S(1)} %shard_map.46), channel_id=1, source_target_pairs={{5,0},{6,1},{7,2},{4,3},{1,4},{2,5},{3,6},{0,7},{13,8},{14,9},{15,... | collective-permute-start | bytes 79880 | tf_op jit(solution)/shard_map/ppermute | solution.py:536
  7.2 2.8 %collective-permute-start = (f32[52,128]{1,0:T(8,128)S(1)}, f32[52,128]{1,0:T(8,128)S(1)}, u32[]{:S(2)}, u32[]{:S(2)}) collective-permute-start(f32[52,128]{1,0:T(8,128)S(1)} %shard_map.46), channel_id=1, source_target_pairs={{4,0},{5,1},{6,2},{7,3},{0,4},{1,5},{2,6},{3,7},{12,8},{13,9},{14,... | collective-permute-start | bytes 79880 | tf_op jit(solution)/shard_map/ppermute | solution.py:536
  11.1 4.9 %collective-permute-start.9 = (f32[112,128]{1,0:T(8,128)S(1)}, f32[112,128]{1,0:T(8,128)S(1)}, u32[]{:S(2)}, u32[]{:S(2)}) collective-permute-start(f32[112,128]{1,0:T(8,128)S(1)} %shard_map.47.refs_1_), channel_id=1, source_target_pairs={{0,28},{4,24},{8,20},{12,16},{16,12},{20,8},{24,4},{28,0},{1,29},{... | collective-permute-start | bytes 172040 | tf_op jit(solution)/shard_map/ppermute | solution.py:558
  13.3 3.7 %collective-permute-start.7 = (f32[112,128]{1,0:T(8,128)S(1)}, f32[112,128]{1,0:T(8,128)S(1)}, u32[]{:S(2)}, u32[]{:S(2)}) collective-permute-start(f32[112,128]{1,0:T(8,128)S(1)} %shard_map.47.refs_1_), channel_id=1, source_target_pairs={{0,20},{4,16},{8,28},{12,24},{16,4},{20,0},{24,12},{28,8},{1,21},{... | collective-permute-start | bytes 172040 | tf_op jit(solution)/shard_map/ppermute | solution.py:558
  13.8 4.8 %collective-permute-start.6 = (f32[112,128]{1,0:T(8,128)S(1)}, f32[112,128]{1,0:T(8,128)S(1)}, u32[]{:S(2)}, u32[]{:S(2)}) collective-permute-start(f32[112,128]{1,0:T(8,128)S(1)} %shard_map.47.refs_1_), channel_id=1, source_target_pairs={{0,8},{4,12},{8,0},{12,4},{16,24},{20,28},{24,16},{28,20},{1,9},{5... | collective-permute-start | bytes 172040 | tf_op jit(solution)/shard_map/ppermute | solution.py:558
  14.3 4.2 %collective-permute-start.5 = (f32[112,128]{1,0:T(8,128)S(1)}, f32[112,128]{1,0:T(8,128)S(1)}, u32[]{:S(2)}, u32[]{:S(2)}) collective-permute-start(f32[112,128]{1,0:T(8,128)S(1)} %shard_map.47.refs_1_), channel_id=1, source_target_pairs={{0,12},{4,8},{8,4},{12,0},{16,28},{20,24},{24,20},{28,16},{1,13},{... | collective-permute-start | bytes 172040 | tf_op jit(solution)/shard_map/ppermute | solution.py:558
  15.2 3.3 %collective-permute-start.4 = (f32[112,128]{1,0:T(8,128)S(1)}, f32[112,128]{1,0:T(8,128)S(1)}, u32[]{:S(2)}, u32[]{:S(2)}) collective-permute-start(f32[112,128]{1,0:T(8,128)S(1)} %shard_map.47.refs_1_), channel_id=1, source_target_pairs={{0,4},{4,0},{8,12},{12,8},{16,20},{20,16},{24,28},{28,24},{1,5},{5... | collective-permute-start | bytes 172040 | tf_op jit(solution)/shard_map/ppermute | solution.py:558
  15.9 2.6 %collective-permute-start.10 = (f32[112,128]{1,0:T(8,128)S(1)}, f32[112,128]{1,0:T(8,128)S(1)}, u32[]{:S(2)}, u32[]{:S(2)}) collective-permute-start(f32[112,128]{1,0:T(8,128)S(1)} %collective-permute-done.9.refs_7_), channel_id=1, source_target_pairs={{0,4},{4,0},{8,12},{12,8},{16,20},{20,16},{24,28},{28,24},{1,5},{5... | collective-permute-start | bytes 172040 | tf_op jit(solution)/shard_map/ppermute | solution.py:558
  16.9 1.6 %collective-permute-start.8 = (f32[112,128]{1,0:T(8,128)S(1)}, f32[112,128]{1,0:T(8,128)S(1)}, u32[]{:S(2)}, u32[]{:S(2)}) collective-permute-start(f32[112,128]{1,0:T(8,128)S(1)} %collective-permute-done.7.refs_5_), channel_id=1, source_target_pairs={{0,4},{4,0},{8,12},{12,8},{16,20},{20,16},{24,28},{28,24},{1,5},{5... | collective-permute-start | bytes 172040 | tf_op jit(solution)/shard_map/ppermute | solution.py:558
